TPU v7x, 32 devices: a whole 2x2x4 slice. The times are simulated.
32 devices in a mesh: seq: 16 (over z, y, x), tp: 2 (over core).
Axes of the slice: x: 2, y: 2, z: 4, core: 2. Of those that a mesh axis runs over, the one named last changes fastest.
Arguments:
- tokens: bfloat16 [8192, 2048], P('seq', 'tp'), may hold values from -6 to 6
- in_weight: bfloat16 [2048, 2, 2048], P(None, None, 'tp'), may hold values from -0.125 to 0.125
- bc_weight: bfloat16 [2048, 256], P(None, 'tp'), may hold values from -0.125 to 0.125
- dt_weight: bfloat16 [2, 2048, 32], P(None, None, 'tp'), may hold values from -0.125 to 0.125
- dt_bias: float32 [2, 32], P(None, 'tp'), may hold values from -2 to 0.5
- decay_rate: float32 [32], P('tp'), may hold values from 1e-05 to 0.5
- skip_gain: float32 [32], P('tp'), may hold values from 0.5 to 300
- out_weight: bfloat16 [2048, 2048], P('tp'), may hold values from -0.1875 to 0.1875
Outputs:
- mixed: bfloat16 [8192, 2048], P('seq', 'tp')
All inputs are finite; a program needn't handle non-finite values.
Results may differ from a plain program's by a relative error of at most 0.018.
Values may be sent and summed in bfloat16 or wider, within the bound.
A program may use at most 128 MiB of HBM per device.

v0:
```python
import jax
import jax.numpy as jnp
from jax import lax
from jax.sharding import PartitionSpec as P

HEAD_DIM = 64
STATE = 128


def carried_in(value, axis, join, neutral, backward):
    count, mine = (lax.axis_size(axis), lax.axis_index(axis))
    pieces = jax.tree.map(lambda part: lax.all_gather(part, axis), value)
    if backward:
        pieces = jax.tree.map(lambda part: part[::-1], pieces)
        mine = count - 1 - mine
    so_far = jax.tree.map(
        lambda part, zero: jnp.full_like(part, 0) + jnp.asarray(zero, part.dtype), value, neutral
    )

    def lap(position, so_far):
        longer = join(so_far, jax.tree.map(lambda part: part[position], pieces))
        return jax.tree.map(lambda new, old: jnp.where(position < mine, new, old), longer, so_far)

    return lax.fori_loop(0, count - 1, lap, so_far)


def combine_states(earlier, later):
    return (earlier[0] + later[0], jnp.exp(later[0])[:, None, None] * earlier[1] + later[1])


def shards(tokens, in_weight, bc_weight, dt_weight, dt_bias, decay_rate, skip_gain, out_weight):
    whole = lax.all_gather(tokens, "tp", axis=1, tiled=True)
    length = whole.shape[0]
    heads_here = decay_rate.shape[0]
    projected = jnp.einsum("td,dkf->tkf", whole, in_weight, preferred_element_type=jnp.float32)
    values = projected[:, 0].astype(jnp.bfloat16).reshape(length, heads_here, HEAD_DIM)
    gates = projected[:, 1].reshape(length, heads_here, HEAD_DIM)
    full_columns = lax.all_gather(bc_weight, "tp", axis=1, tiled=True)
    both = jnp.dot(whole, full_columns, preferred_element_type=jnp.float32).astype(jnp.bfloat16)
    keys = both[:, :STATE]
    queries = both[:, STATE:]
    steps = jax.nn.softplus(
        jnp.einsum("td,kdh->kth", whole, dt_weight, preferred_element_type=jnp.float32)
        + dt_bias[:, None, :]
    )
    forward_steps = steps[0]
    backward_steps = steps[1]
    forward_logs = -decay_rate[None, :] * forward_steps
    backward_logs = -decay_rate[None, :] * backward_steps
    rows = jnp.arange(length, dtype=jnp.int32)[:, None]
    cols = jnp.arange(length, dtype=jnp.int32)[None, :]
    running = (rows >= cols).astype(jnp.float32)
    both_logs = jnp.concatenate([forward_logs, backward_logs], axis=1)
    both_upto = jnp.dot(
        running, both_logs, precision=lax.Precision.HIGHEST, preferred_element_type=jnp.float32
    )
    forward_upto = both_upto[:, :heads_here]
    backward_upto = both_upto[:, heads_here:]
    forward_before = forward_upto - forward_logs
    backward_before = backward_upto - backward_logs
    forward_total = forward_upto[-1]
    backward_total = backward_upto[-1]
    keys_wide = keys.astype(jnp.float32)
    forward_keys = (
        keys_wide[:, None, :]
        * (jnp.exp(forward_total[None, :] - forward_upto) * forward_steps)[:, :, None]
    ).astype(jnp.bfloat16)
    backward_keys = (
        keys_wide[:, None, :] * (jnp.exp(backward_before) * backward_steps)[:, :, None]
    ).astype(jnp.bfloat16)
    forward_state = jnp.einsum(
        "shp,shn->hpn", values, forward_keys, preferred_element_type=jnp.float32
    )
    backward_state = jnp.einsum(
        "shp,shn->hpn", values, backward_keys, preferred_element_type=jnp.float32
    )
    empty = (jnp.zeros_like(forward_total), jnp.zeros_like(forward_state))
    forward_enter = carried_in((forward_total, forward_state), "seq", combine_states, empty, False)[
        1
    ]
    backward_enter = carried_in(
        (backward_total, backward_state), "seq", combine_states, empty, True
    )[1]
    scores = lax.dot_general(
        queries, keys, (((1,), (1,)), ((), ())), preferred_element_type=jnp.float32
    )
    lower_mask = (rows > cols)[None]
    upper_mask = (rows < cols)[None]
    forward_gap = jnp.where(
        lower_mask, forward_before.T[:, :, None] - forward_upto.T[:, None, :], 0.0
    )
    forward_weights = jnp.where(
        lower_mask, scores[None] * jnp.exp(forward_gap) * forward_steps.T[:, None, :], 0.0
    ).astype(jnp.bfloat16)
    backward_gap = jnp.where(
        upper_mask, backward_before.T[:, None, :] - backward_upto.T[:, :, None], 0.0
    )
    backward_weights = jnp.where(
        upper_mask, scores[None] * jnp.exp(backward_gap) * backward_steps.T[:, None, :], 0.0
    ).astype(jnp.bfloat16)
    inner = jnp.einsum("hts,shp->thp", forward_weights, values, preferred_element_type=jnp.float32)
    inner = inner + jnp.einsum(
        "hts,shp->thp", backward_weights, values, preferred_element_type=jnp.float32
    )
    queries_wide = queries.astype(jnp.float32)
    mix = inner + jnp.exp(forward_before)[:, :, None] * jnp.einsum(
        "tn,hpn->thp", queries_wide, forward_enter, precision=lax.Precision.HIGHEST
    )
    mix = mix + jnp.exp(backward_total[None, :] - backward_upto)[:, :, None] * jnp.einsum(
        "tn,hpn->thp", queries_wide, backward_enter, precision=lax.Precision.HIGHEST
    )
    mix = mix + skip_gain[None, :, None] * values.astype(jnp.float32)
    gated = mix * jax.nn.silu(gates)
    power = jnp.mean(gated * gated, axis=-1, keepdims=True)
    hidden = (
        (gated * lax.rsqrt(power + 1e-05))
        .astype(jnp.bfloat16)
        .reshape(length, heads_here * HEAD_DIM)
    )
    partial_terms = jnp.dot(hidden, out_weight, preferred_element_type=jnp.float32)
    return lax.psum_scatter(
        partial_terms.astype(jnp.bfloat16), "tp", scatter_dimension=1, tiled=True
    )


def solution(mesh):
    in_specs = (
        P("seq", "tp"),
        P(None, None, "tp"),
        P(None, "tp"),
        P(None, None, "tp"),
        P(None, "tp"),
        P("tp"),
        P("tp"),
        P("tp", None),
    )
    out_specs = P("seq", "tp")
    return jax.shard_map(shards, mesh=mesh, in_specs=in_specs, out_specs=out_specs, check_vma=False)
```

profile of v0, /device:TPU:0, one launch (start us, length us, event | category | flops | bytes accessed | tf_op | source)
XLA Modules:
  0.0 312.3 jit_solution(13519015528077288300)
XLA Ops:
  8.7 13.5 %all-gather.9.cloned.1.call-done = bf16[512,2048]{1,0:T(8,128)(2,1)} async-done(((bf16[512,1024]{1,0:T(8,128)(2,1)}), bf16[512,2048]{1,0:T(8,128)(2,1)}) %all-gather.9.cloned.1.call-update) | async-done | bytes 2097168 | tf_op jit(solution)/shard_map/all_gather | solution.py:32
  22.2 8.3 %fusion.2 = f32[512,2,1024]{2,0,1:T(8,128)S(1)} fusion(bf16[2048,2,1024]{2,1,0:T(2,128)(2,1)} %param.13, bf16[512,2048]{1,0:T(8,128)(2,1)} %all-gather.9.cloned.1.call-done), kind=kOutput, calls=%fused_computation.8 | convolution fusion | flops 4294967296 | bytes 14680064 | tf_op jit(solution)/shard_map/td,dkf->tkf/dot_general | solution.py:35
  30.6 1.9 copy-done.2
  32.6 1.3 copy.21
  36.0 2.0 convolution_convert_fusion.1
  38.9 2.3 fusion.9
  41.3 2.3 fusion.8
  45.3 1.6 slice-done
  46.9 1.9 copy.22
  48.8 41.0 %all-gather.3 = f32[16,1,16]{2,1,0:T(1,128)S(1)} all-gather(f32[1,1,16]{2,1,0:T(1,128)S(1)} %bitcast.102), channel_id=1, replica_groups=mesh['seq'=16,'tp'=2] {'seq'}, dimensions={0}, use_global_device_ids=true | all-gather | bytes 1088 | tf_op jit(solution)/shard_map/all_gather | solution.py:12
  89.8 35.8 %all-gather.2 = f32[16,1,16]{2,1,0:T(1,128)S(1)} all-gather(f32[1,1,16]{2,1,0:T(1,128)S(1)} %bitcast.101), channel_id=1, replica_groups=mesh['seq'=16,'tp'=2] {'seq'}, dimensions={0}, use_global_device_ids=true | all-gather | bytes 1088 | tf_op jit(solution)/shard_map/all_gather | solution.py:12
  125.6 1.3 fusion.30
  126.9 7.8 %fusion.4 = f32[16,64,512]{2,1,0:T(8,128)} fusion(bf16[512,16,64]{0,2,1:T(8,128)(2,1)} %bitcast.93, f32[16,512]{1,0:T(8,128)S(1)} %get-tuple-element.267, f32[16,512]{1,0:T(8,128)S(1)} %get-tuple-element.260, f32[16,512]{1,0:T(8,128)S(1)} %get-tuple-element.256, f32[512,512]{1,0:T(8,128)S(1)} %fusion.30, pred[512,512]{1,0:T(8,128)(4,1)} %iota_compare_fusion.2), kind=kOutput, calls=%fused_computation.10 | convolution fusion | flops 562036736 | bytes 4554752 | tf_op jit(solution)/shard_map/hts,shp->thp/dot_general | solution.py:101
  134.7 5.9 %fusion.5 = f32[16,64,512]{2,1,0:T(8,128)} fusion(bf16[512,16,64]{0,2,1:T(8,128)(2,1)S(1)} %bitcast.96, f32[16,512]{1,0:T(8,128)S(1)} %get-tuple-element.266, f32[16,512]{1,0:T(8,128)S(1)} %get-tuple-element.261, f32[16,512]{1,0:T(8,128)S(1)} %get-tuple-element.263, f32[512,512]{1,0:T(8,128)S(1)} %fusion.30, pred[512,512]{1,0:T(8,128)(4,1)S(1)} %copy-done.9), kind=kOutput, calls=%fused_computation.11 | convolution fusion | flops 562036736 | bytes 4554752 | tf_op jit(solution)/shard_map/hts,shp->thp/dot_general | solution.py:102
  140.6 15.0 %all-gather.15.cloned.1.call-done = f32[256,64,128]{2,1,0:T(8,128)} async-done(((f32[16,64,128]{2,1,0:T(8,128)}), f32[256,64,128]{2,1,0:T(8,128)}) %all-gather.15.cloned.1.call-update) | async-done | bytes 8388624 | tf_op jit(solution)/shard_map/all_gather | solution.py:12
  155.6 8.3 %rev.7 = f32[16,16,64,128]{3,2,1,0:T(8,128)} reverse(f32[16,16,64,128]{3,2,1,0:T(8,128)} %bitcast.90), dimensions={0} | reverse | bytes 16777216 | tf_op jit(solution)/shard_map/rev | solution.py:14
  163.9 18.3 %while.29 = (s32[]{:T(128)}, f32[16,64,128]{2,1,0:T(8,128)S(1)}, s32[]{:T(128)}, f32[16,16]{1,0:T(8,128)S(1)}, f32[16,16,64,128]{3,2,1,0:T(8,128)}, /*index=5*/s32[]{:T(128)}, s32[]{:T(128)}) while((s32[]{:T(128)}, f32[16,64,128]{2,1,0:T(8,128)S(1)}, s32[]{:T(128)}, f32[16,16]{1,0:T(8,128)S(1)}, f32[16,16,64,128]{3,2,1,0:T(8,128)}, ...), condition=%wide.region_3.4_spmd.clone, body=%wide.region_2.3_spmd.clone.sunk | while | flops 524292 | bytes 1573169 | solution.py:24
  163.9 1.2 fusion.60
  165.1 1.2 fusion.60
  166.4 1.2 fusion.60
  167.6 1.2 fusion.60
  168.8 1.2 fusion.60
  170.0 1.2 fusion.60
  171.3 1.2 fusion.60
  172.5 1.2 fusion.60
  173.7 1.2 fusion.60
  174.9 1.2 fusion.60
  176.1 1.2 fusion.60
  177.4 1.2 fusion.60
  178.6 1.2 fusion.60
  179.8 1.2 fusion.60
  181.0 1.2 fusion.60
  182.2 87.1 %all-gather.13.cloned.1.call-done = f32[256,64,128]{2,1,0:T(8,128)} async-done(((f32[16,64,128]{2,1,0:T(8,128)}), f32[256,64,128]{2,1,0:T(8,128)}) %all-gather.13.cloned.1.call-update) | async-done | bytes 8388624 | tf_op jit(solution)/shard_map/all_gather | solution.py:12
  269.3 18.3 %while.28 = (s32[]{:T(128)}, f32[16,64,128]{2,1,0:T(8,128)S(1)}, s32[]{:T(128)}, f32[16,16]{1,0:T(8,128)S(1)}, f32[16,16,64,128]{3,2,1,0:T(8,128)}, /*index=5*/s32[]{:T(128)}, s32[]{:T(128)}) while((s32[]{:T(128)}, f32[16,64,128]{2,1,0:T(8,128)S(1)}, s32[]{:T(128)}, f32[16,16]{1,0:T(8,128)S(1)}, f32[16,16,64,128]{3,2,1,0:T(8,128)}, ...), condition=%wide.region_1.2_spmd.clone, body=%wide.region_0.1_spmd.clone.sunk | while | flops 524292 | bytes 1573169 | solution.py:24
  269.3 1.2 fusion.59
  270.6 1.2 fusion.59
  271.8 1.2 fusion.59
  273.0 1.2 fusion.59
  279.1 1.2 fusion.59
  280.3 1.2 fusion.59
  281.5 1.2 fusion.59
  282.8 1.2 fusion.59
  284.0 1.2 fusion.59
  285.2 1.2 fusion.59
  286.4 1.2 fusion.59
  289.2 4.4 %multiply_reduce_fusion = (f32[512,16]{0,1:T(8,128)S(1)}, f32[512,16,64]{0,2,1:T(8,128)S(1)}) fusion(f32[512,16,64]{0,2,1:T(8,128)S(1)} %bitcast.91, bf16[512,16,64]{0,2,1:T(8,128)(2,1)S(1)} %bitcast.97, f32[16]{0:T(128)S(1)} %copy-done.12, f32[16,64,128]{2,1,0:T(8,128)S(1)} %get-tuple-element.194, bf16[512,256]{1,0:T(8,128)(2,1)S(1)} %copy-done.8, ...), kind=kOutput, calls=%fused_computation.28 | convolution fusion | flops 813162496 | bytes 12288512 | tf_op jit(solution)/shard_map/tn,hpn->thp/dot_general | solution.py:109
  294.0 3.8 %convolution_convert_fusion = bf16[512,2048]{1,0:T(8,128)(2,1)} fusion(bf16[512,1024]{0,1:T(8,128)(2,1)S(1)} %bitcast.92, bf16[1024,2048]{1,0:T(8,128)(2,1)S(1)} %copy-done.11), kind=kOutput, calls=%fused_computation.16 | convolution fusion | flops 2148532224 | bytes 7340032 | tf_op jit(solution)/shard_map/dot_general | solution.py:120
  297.8 8.0 %reduce-scatter.2.cloned.1.call-done = bf16[512,1024]{1,0:T(8,128)(2,1)} async-done(((bf16[512,2048]{1,0:T(8,128)(2,1)}), bf16[512,1024]{1,0:T(8,128)(2,1)}) %reduce-scatter.2.cloned.1.call-update) | async-done | bytes 1048592 | tf_op jit(solution)/shard_map/reduce_scatter | solution.py:121
  (88 shorter events, 13.8 us)
Async XLA Ops:
  6.5 27.4 %copy-start = (bf16[2,2048,16]{1,2,0:T(8,128)(2,1)S(1)}, bf16[2,2048,16]{1,2,0:T(8,128)(2,1)}, u32[]{:S(2)}) copy-start(bf16[2,2048,16]{1,2,0:T(8,128)(2,1)} %param.15) | copy-start | bytes 393220
  6.5 15.7 %all-gather.9.cloned.1.call-start = ((), (), s32[]{:S(2)}) async-start(), calls=%async_computation.1 | async-start | bytes 3145728 | tf_op jit(solution)/shard_map/all_gather | solution.py:32
  7.3 28.8 %all-gather.11.cloned.1.call-start = ((), (), s32[]{:S(2)}) async-start(), calls=%async_computation.2 | async-start | bytes 1572864 | tf_op jit(solution)/shard_map/all_gather | solution.py:38
  8.0 147.6 %all-gather.15.cloned.1.call-start = ((), (), s32[]{:S(2)}) async-start(), calls=%async_computation.5 | async-start | bytes 8912896 | tf_op jit(solution)/shard_map/all_gather | solution.py:12
  30.5 1.9 copy-start.2
  32.5 2.0 copy-start.4
  32.5 2.0 copy-start.10
  36.0 2.9 copy-start.5
  38.1 0.7 copy-start.7
  41.2 228.0 %all-gather.13.cloned.1.call-start = ((), (), s32[]{:S(2)}) async-start(), calls=%async_computation.4 | async-start | bytes 8912896 | tf_op jit(solution)/shard_map/all_gather | solution.py:12
  43.6 262.1 %reduce-scatter.2.cloned.1.call-start = ((), (), s32[]{:S(2)}) async-start(), calls=%async_computation.3 | async-start | bytes 3145728 | tf_op jit(solution)/shard_map/reduce_scatter | solution.py:121
  45.3 1.6 slice-start
  126.9 7.8 %copy-start.6 = (bf16[512,1,1024]{0,2,1:T(8,128)(2,1)S(1)}, bf16[512,1,1024]{0,2,1:T(8,128)(2,1)}, u32[]{:S(2)}) copy-start(bf16[512,1,1024]{0,2,1:T(8,128)(2,1)} %copy.21) | copy-start | bytes 3145732
  126.9 7.8 %copy-start.9 = (pred[512,512]{1,0:T(8,128)(4,1)S(1)}, pred[512,512]{1,0:T(8,128)(4,1)}, u32[]{:S(2)}) copy-start(pred[512,512]{1,0:T(8,128)(4,1)} %iota_compare_fusion) | copy-start | bytes 786436
  269.3 18.3 %copy-start.8 = (bf16[512,256]{1,0:T(8,128)(2,1)S(1)}, bf16[512,256]{1,0:T(8,128)(2,1)}, u32[]{:S(2)}) copy-start(bf16[512,256]{1,0:T(8,128)(2,1)} %copy-done.7) | copy-start | bytes 786436
  287.6 1.6 copy-start.3
  287.6 1.6 copy-start.12
  289.2 4.8 %copy-start.11 = (bf16[1024,2048]{1,0:T(8,128)(2,1)S(1)}, bf16[1024,2048]{1,0:T(8,128)(2,1)}, u32[]{:S(2)}) copy-start(bf16[1024,2048]{1,0:T(8,128)(2,1)} %param.19) | copy-start | bytes 12582916
  294.0 11.8 %copy-start.1 = (bf16[2,2048,16]{1,2,0:T(8,128)(2,1)S(1)}, bf16[2,2048,16]{1,2,0:T(8,128)(2,1)}, u32[]{:S(2)}) copy-start(bf16[2,2048,16]{1,2,0:T(8,128)(2,1)} %param.15) | copy-start | bytes 393220
Sparse Core Ops, SparseCore 0:
  8.9 13.2 all-gather.8
  23.7 10.1 all-gather.10
  41.4 114.1 all-gather.14
  158.2 111.0 all-gather.12
  297.9 7.7 reduce-scatter.1
where the time goes:
time: 314 us; the launch traced here: 312 us
  waiting for transfers between devices  125 us (40%)
  blocking collectives  76.8 us (24%)
  matrix products  40.4 us (13%)
  other arithmetic  38.1 us (12%)
  local copies, waits for them, and re-layouts  17.5 us (6%)
  between operations  13.4 us (4%)
    all_gather x2, waiting for transfers between devices, carried_in(): pieces = jax.tree.map(lambda part: lax.all_gather(part, axis), value)  102 us
    all_gather x2, blocking collectives, carried_in(): pieces = jax.tree.map(lambda part: lax.all_gather(part, axis), value)  76.8 us
    select_n x30, other arithmetic, lap(): jnp.where(position < mine, new, old)  35.3 us
    all_gather x1, waiting for transfers between devices, shards(): whole = lax.all_gather(tokens, 'tp', axis=1, tiled=True)  13.5 us
    dot_general x1, matrix products, shards(): jnp.einsum('td,dkf->tkf', whole, in_weight, preferred_element_type=jnp.fl...  8.32 us
    rev x2, local copies, waits for them, and re-layouts, carried_in(): pieces = jax.tree.map(lambda part: part[::-1], pieces)  8.31 us
    reduce_scatter x1, waiting for transfers between devices, shards(): lax.psum_scatter(partial_terms.astype(jnp.bfloat16), 'tp', scatter_dimens...  7.95 us
    dot_general x1, matrix products, shards(): jnp.einsum('hts,shp->thp', forward_weights, values, preferred_element_typ...  7.77 us
  transfers between devices with their start and end apart: 5, of which 4 were waited for; matrix products, arithmetic and copies ran while one was open for 19% of the time, Pallas kernels for 0%

commit v1 on v0

v1 whole, which is shorter than its diff:
```python
import functools

import jax
import jax.numpy as jnp
from jax import lax
from jax.experimental import pallas as pl
from jax.experimental.pallas import tpu as pltpu
from jax.sharding import PartitionSpec as P

HEAD_DIM = 64
STATE = 128
CHUNK = 128
GROUP = 4
VMEM_LIMIT = 48 * 1024 * 1024
F32 = jnp.float32
BF16 = jnp.bfloat16
HIGH = lax.Precision.HIGHEST


def dot(a, b, contract=((1,), (0,)), precision=None):
    return lax.dot_general(
        a, b, (contract, ((), ())), precision=precision, preferred_element_type=F32
    )


def split_wide(value):
    high = value.astype(BF16)
    return jnp.concatenate([high, (value - high.astype(F32)).astype(BF16)], axis=1)


def spread_matrix(count, dtype, copies=1):
    rows = lax.broadcasted_iota(jnp.int32, (copies * count, count * HEAD_DIM), 0)
    lanes = lax.broadcasted_iota(jnp.int32, (copies * count, count * HEAD_DIM), 1)
    return (lax.rem(rows, count) == lanes // HEAD_DIM).astype(dtype)


def chunk_decays(raw, rate):
    steps = jnp.maximum(raw, 0.0) + jnp.log1p(jnp.exp(-jnp.abs(raw)))
    logs = -rate * steps
    rows = lax.broadcasted_iota(jnp.int32, (CHUNK, CHUNK), 0)
    cols = lax.broadcasted_iota(jnp.int32, (CHUNK, CHUNK), 1)
    running = (rows >= cols).astype(F32)
    upto = dot(running, logs, precision=HIGH)
    return steps, upto, upto - logs


def states_kernel(proj_ref, both_ref, raw_ref, rate_ref, local_ref, send_ref, total_ref, sums):
    heads2 = raw_ref.shape[1]
    heads = heads2 // 2
    width = heads * HEAD_DIM
    chunks = raw_ref.shape[0] // CHUNK
    spread = spread_matrix(heads2, BF16, 2)
    spread_wide = spread_matrix(heads2, F32)
    forward = lax.broadcasted_iota(jnp.int32, (CHUNK, heads2), 1) < heads
    totals = []
    for c in range(chunks):
        rows = pl.ds(c * CHUNK, CHUNK)
        steps, upto, before = chunk_decays(raw_ref[rows, :], rate_ref[...])
        last = upto[CHUNK - 1 : CHUNK, :]
        weight = jnp.exp(jnp.where(forward, last - upto, before)) * steps
        weight = dot(split_wide(weight), spread)
        values = proj_ref[0, rows, :].astype(BF16).astype(F32)
        weighted = (jnp.concatenate([values, values], axis=1) * weight).astype(BF16)
        sums[c] = dot(both_ref[rows, :STATE], weighted, ((0,), (0,)))
        totals.append(dot(jnp.broadcast_to(last, (8, heads2)), spread_wide, precision=HIGH))
    block = functools.reduce(jnp.add, totals)
    quarter = width // GROUP
    for way in range(2):
        side = slice(way * width, (way + 1) * width)
        order = range(chunks) if way == 0 else range(chunks - 1, -1, -1)
        carry = jnp.zeros((STATE, width), F32)
        for c in order:
            local_ref[c, :, side] = carry.astype(BF16)
            carry = jnp.exp(totals[c][:1, side]) * carry + sums[c, :, side]
        for g in range(GROUP):
            part = slice(g * quarter, (g + 1) * quarter)
            send_ref[g, way] = carry[:, part].astype(BF16)
            total_ref[g, way] = block[:, side][:, part]


def carry_kernel(
    outer,
    send_ref,
    total_ref,
    enter_ref,
    got,
    got_total,
    inner,
    group,
    group_total,
    far,
    far_total,
    back,
    landed,
    send1,
    recv1,
    send2,
    recv2,
    send3,
    recv3,
):
    seq = lax.axis_index("seq")
    z, g = seq // GROUP, seq % GROUP

    def peer(zz, gg):
        return {"seq": zz * GROUP + gg}

    barrier = pltpu.get_barrier_semaphore()
    for d in range(1, GROUP):
        pl.semaphore_signal(
            barrier, inc=1, device_id=peer(z, (g + d) % GROUP), device_id_type=pl.DeviceIdType.MESH
        )
    for d in range(1, outer):
        pl.semaphore_signal(
            barrier, inc=1, device_id=peer((z + d) % outer, g), device_id_type=pl.DeviceIdType.MESH
        )
    pl.semaphore_wait(barrier, GROUP - 1 + outer - 1)

    def push(source, target, sends, recvs, slot, where):
        copy = pltpu.make_async_remote_copy(
            src_ref=source,
            dst_ref=target,
            send_sem=sends.at[slot],
            recv_sem=recvs.at[slot],
            device_id=where,
            device_id_type=pl.DeviceIdType.MESH,
        )
        copy.start()
        return copy

    copies = []
    for d in range(1, GROUP):
        to = (g + d) % GROUP
        copies.append(push(total_ref.at[to], got_total.at[g], send1, recv1, 2 * d - 1, peer(z, to)))
        copies.append(push(send_ref.at[to], got.at[g], send1, recv1, 2 * d - 2, peer(z, to)))
    got[g] = send_ref[g]
    got_total[g] = total_ref[g]
    for copy in copies:
        copy.wait()
    before = [[None] * GROUP, [None] * GROUP]
    for way in range(2):
        order = range(GROUP) if way == 0 else range(GROUP - 1, -1, -1)
        carry = jnp.zeros(got.shape[2:], F32)
        passed = jnp.zeros(got_total.shape[2:], F32)
        for s in order:
            inner[s, way] = carry
            before[way][s] = jnp.exp(passed[:1])
            carry = jnp.exp(got_total[s, way][:1]) * carry + got[s, way].astype(F32)
            passed = passed + got_total[s, way]
        group[way] = carry.astype(BF16)
        group_total[way] = passed

    copies = []
    for d in range(1, outer):
        way = (z + d) // outer
        to = peer((z + d) % outer, g)
        copies.append(push(group_total.at[way], far_total.at[z], send2, recv2, 2 * d - 1, to))
        copies.append(push(group.at[way], far.at[z], send2, recv2, 2 * d - 2, to))
    far[z] = jnp.zeros(far.shape[1:], BF16)
    far_total[z] = jnp.zeros(far_total.shape[1:], F32)
    for copy in copies:
        copy.wait()
    for way in range(2):
        order = range(outer) if way == 0 else range(outer - 1, -1, -1)
        carry = jnp.zeros(far.shape[1:], F32)
        for s in order:
            longer = jnp.exp(far_total[s][:1]) * carry + far[s].astype(F32)
            carry = jnp.where(s < z if way == 0 else s > z, longer, carry)
        for s in range(GROUP):
            back[s, way] = (inner[s, way] + before[way][s] * carry).astype(BF16)

    copies = []
    for d in range(1, GROUP):
        to = (g + d) % GROUP
        copies.append(push(back.at[to], landed.at[g], send3, recv3, d - 1, peer(z, to)))
    landed[g] = back[g]
    for copy in copies:
        copy.wait()
    enter_ref[...] = landed[...]


def mix_kernel(proj_ref, both_ref, raw_ref, rate_ref, gain_ref, local_ref, enter_ref, out_ref, wide):
    heads2 = raw_ref.shape[1]
    heads = heads2 // 2
    width = heads * HEAD_DIM
    chunks = raw_ref.shape[0] // CHUNK
    quarter = width // GROUP
    for g in range(GROUP):
        for way in range(2):
            start = way * width + g * quarter
            wide[:, start : start + quarter] = enter_ref[g, way].astype(F32)
    spread = spread_matrix(heads2, BF16, 2)
    spread_one = spread_matrix(heads, BF16, 2)
    spread_wide = spread_matrix(heads2, F32)
    forward = lax.broadcasted_iota(jnp.int32, (CHUNK, heads2), 1) < heads
    rows_of = lax.broadcasted_iota(jnp.int32, (CHUNK, CHUNK), 0)
    cols_of = lax.broadcasted_iota(jnp.int32, (CHUNK, CHUNK), 1)
    lower = rows_of > cols_of
    on_line = rows_of == cols_of
    first_half = lax.broadcasted_iota(jnp.int32, (CHUNK, 2 * HEAD_DIM), 1) < HEAD_DIM
    decays = []
    for c in range(chunks):
        decays.append(chunk_decays(raw_ref[c * CHUNK : (c + 1) * CHUNK, :], rate_ref[...]))
    lasts = [upto[CHUNK - 1 : CHUNK, :] for _, upto, _ in decays]
    for c in range(chunks):
        rows = slice(c * CHUNK, (c + 1) * CHUNK)
        steps, upto, before = decays[c]
        last = lasts[c]
        column = jnp.where(forward, before, -upto)
        row = (jnp.where(forward, -upto, before) + jnp.log(steps)).T
        keys = both_ref[rows, :STATE]
        queries = both_ref[rows, STATE:]
        scores = dot(queries, keys, ((1,), (1,)))
        values = proj_ref[0, rows, :].astype(BF16)
        pieces = []
        for pair in range(heads // 2):
            weights = []
            for h in (2 * pair, 2 * pair + 1):
                power = jnp.where(
                    lower,
                    column[:, h : h + 1] + row[h : h + 1, :],
                    column[:, heads + h : heads + h + 1] + row[heads + h : heads + h + 1, :],
                )
                power = jnp.where(on_line, -jnp.inf, power)
                weights.append((scores * jnp.exp(power)).astype(BF16))
            both_values = values[:, pair * 2 * HEAD_DIM : (pair + 1) * 2 * HEAD_DIM]
            zero = jnp.zeros_like(both_values)
            stacked = jnp.concatenate(
                [
                    jnp.where(first_half, both_values, zero),
                    jnp.where(first_half, zero, both_values),
                ],
                axis=0,
            )
            pieces.append(dot(jnp.concatenate(weights, axis=1), stacked))
        mix = jnp.concatenate(pieces, axis=1)
        passed = jnp.zeros((1, heads2), F32)
        for other in range(chunks):
            if other < c:
                passed = passed + jnp.where(forward[:1], lasts[other], 0.0)
            if other > c:
                passed = passed + jnp.where(forward[:1], 0.0, lasts[other])
        passed = dot(jnp.broadcast_to(passed, (8, heads2)), spread_wide, precision=HIGH)[:1]
        entering = local_ref[c].astype(F32) + jnp.exp(passed) * wide[...]
        reach = dot(queries, entering.astype(BF16))
        scale = jnp.exp(jnp.where(forward, before, last - upto))
        reach = reach * dot(split_wide(scale), spread)
        mix = mix + reach[:, :width] + reach[:, width:]
        mix = mix + gain_ref[...] * values.astype(F32)
        gates = proj_ref[1, rows, :]
        gated = mix * (gates / (1.0 + jnp.exp(-gates)))
        square = gated * gated
        high = square.astype(BF16)
        low = (square - high.astype(F32)).astype(BF16)
        unit = spread_one[:heads]
        power = dot(high, unit, ((1,), (1,))) + dot(low, unit, ((1,), (1,)))
        norm = lax.rsqrt(power * (1.0 / HEAD_DIM) + 1e-05)
        out_ref[rows, :] = (gated * dot(split_wide(norm), spread_one)).astype(BF16)


def shards(tokens, in_weight, bc_weight, dt_weight, dt_bias, decay_rate, skip_gain, out_weight):
    heads = decay_rate.shape[0]
    width = heads * HEAD_DIM
    quarter = width // GROUP
    outer = lax.axis_size("seq") // GROUP
    whole = lax.all_gather(tokens, "tp", axis=1, tiled=True)
    length = whole.shape[0]
    chunks = length // CHUNK
    full_columns = lax.all_gather(bc_weight, "tp", axis=1, tiled=True)
    projected = jnp.einsum("td,dkf->ktf", whole, in_weight, preferred_element_type=F32)
    both = jnp.dot(whole, full_columns, preferred_element_type=F32).astype(BF16)
    raw = jnp.einsum("td,kdh->tkh", whole, dt_weight, preferred_element_type=F32)
    raw = (raw + dt_bias[None]).reshape(length, 2 * heads)
    rate = jnp.concatenate([decay_rate, decay_rate])[None, :]
    gain = jnp.repeat(skip_gain, HEAD_DIM)[None, :]
    params = pltpu.CompilerParams(vmem_limit_bytes=VMEM_LIMIT)
    vmem = pl.BlockSpec(memory_space=pltpu.VMEM)
    local, send, total = pl.pallas_call(
        states_kernel,
        out_shape=(
            jax.ShapeDtypeStruct((chunks, STATE, 2 * width), BF16),
            jax.ShapeDtypeStruct((GROUP, 2, STATE, quarter), BF16),
            jax.ShapeDtypeStruct((GROUP, 2, 8, quarter), F32),
        ),
        grid=(1,),
        in_specs=[
            pl.BlockSpec((1, length, width), lambda i: (0, 0, 0)),
            pl.BlockSpec((length, 2 * STATE), lambda i: (0, 0)),
            pl.BlockSpec((length, 2 * heads), lambda i: (0, 0)),
            pl.BlockSpec((1, 2 * heads), lambda i: (0, 0)),
        ],
        out_specs=(vmem, vmem, vmem),
        scratch_shapes=[pltpu.VMEM((chunks, STATE, 2 * width), F32)],
        compiler_params=params,
        name="block_states",
    )(projected, both, raw, rate)
    enter = pl.pallas_call(
        functools.partial(carry_kernel, outer),
        out_shape=jax.ShapeDtypeStruct((GROUP, 2, STATE, quarter), BF16),
        in_specs=[vmem, vmem],
        out_specs=vmem,
        scratch_shapes=[
            pltpu.VMEM((GROUP, 2, STATE, quarter), BF16),
            pltpu.VMEM((GROUP, 2, 8, quarter), F32),
            pltpu.VMEM((GROUP, 2, STATE, quarter), F32),
            pltpu.VMEM((2, STATE, quarter), BF16),
            pltpu.VMEM((2, 8, quarter), F32),
            pltpu.VMEM((outer, STATE, quarter), BF16),
            pltpu.VMEM((outer, 8, quarter), F32),
            pltpu.VMEM((GROUP, 2, STATE, quarter), BF16),
            pltpu.VMEM((GROUP, 2, STATE, quarter), BF16),
            pltpu.SemaphoreType.DMA((2 * GROUP - 2,)),
            pltpu.SemaphoreType.DMA((2 * GROUP - 2,)),
            pltpu.SemaphoreType.DMA((2 * outer - 2,)),
            pltpu.SemaphoreType.DMA((2 * outer - 2,)),
            pltpu.SemaphoreType.DMA((GROUP - 1,)),
            pltpu.SemaphoreType.DMA((GROUP - 1,)),
        ],
        compiler_params=pltpu.CompilerParams(
            vmem_limit_bytes=VMEM_LIMIT, collective_id=0, has_side_effects=True
        ),
        name="carry_states",
    )(send, total)
    hidden = pl.pallas_call(
        mix_kernel,
        out_shape=jax.ShapeDtypeStruct((length, width), BF16),
        in_specs=[vmem] * 7,
        out_specs=vmem,
        scratch_shapes=[pltpu.VMEM((STATE, 2 * width), F32)],
        compiler_params=params,
        name="mix_chunks",
    )(projected, both, raw, rate, gain, local, enter)
    partial_terms = jnp.dot(hidden, out_weight, preferred_element_type=F32)
    return lax.psum_scatter(partial_terms.astype(BF16), "tp", scatter_dimension=1, tiled=True)


def solution(mesh):
    in_specs = (
        P("seq", "tp"),
        P(None, None, "tp"),
        P(None, "tp"),
        P(None, None, "tp"),
        P(None, "tp"),
        P("tp"),
        P("tp"),
        P("tp", None),
    )
    out_specs = P("seq", "tp")
    return jax.shard_map(shards, mesh=mesh, in_specs=in_specs, out_specs=out_specs, check_vma=False)
```

time: 314 us -> 108 us (0.34)
  waiting for transfers between devices: 125 us -> 32 us
  blocking collectives: 76.8 us -> 0 us
  Pallas kernels: 0 us -> 42.1 us
  other arithmetic: 38.1 us -> 0.88 us
  matrix products: 40.4 us -> 18.6 us
  local copies, waits for them, and re-layouts: 17.5 us -> 0.96 us
    all_gather x2 -> x0, waiting for transfers between devices: 102 us -> none  [carried_in(): pieces = jax.tree.map(lambda part: lax.all_gather(part, axis), value)]
    all_gather x2 -> x0, blocking collectives: 76.8 us -> none  [carried_in(): pieces = jax.tree.map(lambda part: lax.all_gather(part, axis), value)]
    pallas_call x0 -> x3, Pallas kernels: none -> 42.1 us  [the longest x1 25.9 us: shards(): pl.pallas_call(functools.partial(carry_kernel, outer), out_shape=jax.Shap...]
    select_n x30 -> x0, other arithmetic: 35.3 us -> none  [lap(): jnp.where(position < mine, new, old)]
    dot_general x12 -> x3, matrix products: 40.4 us -> 16.2 us  [the longest x1 10.6 us: shards(): jnp.einsum('td,dkf->ktf', whole, in_weight, preferred_element_type=F32)]
    all_gather x1, waiting for transfers between devices: 0.02 us -> 9.04 us  [shards(): full_columns = lax.all_gather(bc_weight, 'tp', axis=1, tiled=True)]
    rev x2 -> x0, local copies, waits for them, and re-layouts: 8.31 us -> none  [carried_in(): pieces = jax.tree.map(lambda part: part[::-1], pieces)]
    slice x6 -> x0, local copies, waits for them, and re-layouts: 5.14 us -> none  [the longest x3 3.48 us: shards(): gates = projected[:, 1].reshape(length, heads_here, HEAD_DIM)]
  transfers between devices with their start and end apart: 5 -> 3, of which waited for: 4 -> 3; matrix products, arithmetic and copies ran while one was open for 19% -> 4% of each run, Pallas kernels for 0% -> 0%
where the time goes in v1:
time: 108 us
  Pallas kernels  42.1 us (39%)
  waiting for transfers between devices  32 us (30%)
  matrix products  18.6 us (17%)
  between operations  13.2 us (12%)
    pallas_call x1, Pallas kernels, shards(): pl.pallas_call(functools.partial(carry_kernel, outer), out_shape=jax.Shap...  25.9 us
    all_gather x1, waiting for transfers between devices, shards(): whole = lax.all_gather(tokens, 'tp', axis=1, tiled=True)  12.6 us
    pallas_call x1, Pallas kernels, shards(): pl.pallas_call(mix_kernel, out_shape=jax.ShapeDtypeStruct((length, width)...  10.9 us
    dot_general x1, matrix products, shards(): jnp.einsum('td,dkf->ktf', whole, in_weight, preferred_element_type=F32)  10.6 us
    all_gather x1, waiting for transfers between devices, shards(): full_columns = lax.all_gather(bc_weight, 'tp', axis=1, tiled=True)  9.04 us
    reduce_scatter x1, waiting for transfers between devices, shards(): lax.psum_scatter(partial_terms.astype(BF16), 'tp', scatter_dimension=1, t...  8.9 us
    pallas_call x1, Pallas kernels, shards(): pl.pallas_call(states_kernel, out_shape=(jax.ShapeDtypeStruct((chunks, ST...  5.29 us
    dot_general x1, matrix products, shards(): partial_terms = jnp.dot(hidden, out_weight, preferred_element_type=F32)  3.67 us
  transfers between devices with their start and end apart: 3, of which 3 were waited for; matrix products, arithmetic and copies ran while one was open for 4% of the time, Pallas kernels for 0%

profile of v1, /device:TPU:0, one launch (start us, length us, event | category | flops | bytes accessed | tf_op | source)
XLA Modules:
  0.0 107.7 jit_solution(899817144424236698)
XLA Ops:
  6.5 0.0 copy-start
  6.5 0.0 copy-start.2
  6.5 0.0 all-gather.3.cloned.1.call-start
  6.5 0.7 all-gather.3.cloned.1.call-update
  7.3 0.0 all-gather.5.cloned.1.call-start
  7.3 0.7 all-gather.5.cloned.1.call-update
  8.0 0.0 reduce-scatter.2.cloned.1.call-start
  8.1 0.7 broadcast_in_dim.8
  8.8 0.1 broadcast_in_dim_reshape.3.gain_ref
  8.9 0.8 maximum_bitcast_fusion.rate_ref
  9.7 12.6 %all-gather.3.cloned.1.call-done = bf16[512,2048]{1,0:T(8,128)(2,1)} async-done(((bf16[512,1024]{1,0:T(8,128)(2,1)}), bf16[512,2048]{1,0:T(8,128)(2,1)}) %all-gather.3.cloned.1.call-update) | async-done | bytes 2097168 | tf_op jit(solution)/shard_map/all_gather | solution.py:266
  22.3 0.0 copy-done
  22.3 0.0 copy-start.1
  22.3 2.5 %fusion.6 = f32[512,32]{0,1:S(1)} fusion(bf16[512,2048]{1,0:T(8,128)(2,1)} %all-gather.3.cloned.1.call-done, bf16[2048,32]{0,1:T(8,128)(2,1)S(1)} %bitcast.18), kind=kOutput, calls=%fused_computation.8 | convolution fusion | flops 67108864 | bytes 2293760
  24.7 0.0 copy-done.2
  24.7 0.1 broadcast_add_fusion
  24.8 0.1 copy.15.raw_ref
  25.0 9.0 %all-gather.5.cloned.1.call-done = bf16[2048,256]{1,0:T(8,128)(2,1)} async-done(((bf16[2048,128]{1,0:T(8,128)(2,1)}), bf16[2048,256]{1,0:T(8,128)(2,1)}) %all-gather.5.cloned.1.call-update) | async-done | bytes 1048592 | tf_op jit(solution)/shard_map/all_gather | solution.py:269
  34.0 0.0 copy-done.1
  34.0 1.9 %convolution_convert_fusion.1.both_ref = bf16[512,256]{1,0:T(8,128)(2,1)S(1)} fusion(bf16[512,2048]{1,0:T(8,128)(2,1)S(1)} %copy-done.1, bf16[2048,256]{1,0:T(8,128)(2,1)} %all-gather.5.cloned.1.call-done), kind=kOutput, calls=%fused_computation.5 | convolution fusion | flops 537001984 | bytes 3407872 | tf_op jit(solution)/shard_map/dot_general | solution.py:271
  35.9 10.6 %fusion.2.proj_ref = f32[2,512,1024]{2,1,0:T(8,128)} fusion(bf16[2048,2,1024]{2,1,0:T(2,128)(2,1)} %param.9, bf16[512,2048]{1,0:T(8,128)(2,1)S(1)} %copy-done.1), kind=kOutput, calls=%fused_computation.3 | convolution fusion | flops 4294967296 | bytes 14680064 | tf_op jit(solution)/shard_map/td,dkf->ktf/dot_general | solution.py:270
  46.5 5.3 %block_states.1 = (bf16[4,128,2048]{2,1,0:T(8,128)(2,1)S(1)}, bf16[4,2,128,256]{3,2,1,0:T(8,128)(2,1)S(1)}, f32[4,2,8,256]{3,2,1,0:T(8,128)S(1)}) custom-call(f32[2,512,1024]{2,1,0:T(8,128)} %fusion.2.proj_ref, bf16[512,256]{1,0:T(8,128)(2,1)S(1)} %convolution_convert_fusion.1.both_ref, f32[512,32]{1,0:T(8,128)S(1)} %copy.15.raw_ref, ...), custom_call_target="tpu_custom_call" | custom-call | tf_op jit(solution)/shard_map/block_states/pallas_call | solution.py:278
  51.8 25.9 %carry_states.1.enter_ref = bf16[4,2,128,256]{3,2,1,0:T(8,128)(2,1)S(1)} custom-call(bf16[4,2,128,256]{3,2,1,0:T(8,128)(2,1)S(1)} %get-tuple-element.9.send_ref, f32[4,2,8,256]{3,2,1,0:T(8,128)S(1)} %get-tuple-element.10.total_ref), custom_call_target="tpu_custom_call" | custom-call | tf_op jit(solution)/shard_map/carry_states/pallas_call | solution.py:297
  77.7 0.0 copy-start.3
  77.7 10.9 %mix_chunks.1 = bf16[512,1024]{1,0:T(8,128)(2,1)S(1)} custom-call(f32[2,512,1024]{2,1,0:T(8,128)} %fusion.2.proj_ref, bf16[512,256]{1,0:T(8,128)(2,1)S(1)} %convolution_convert_fusion.1.both_ref, f32[512,32]{1,0:T(8,128)S(1)} %copy.15.raw_ref, f32[1,32]{1,0:T(1,128)S(1)} %maximum_bitcast_fusion.rate_ref, f32[1,1024]{1,0:T(1,128)S(1)} %broadcast_in_dim_reshape.3.gain_ref, ...), custom_call_target="tpu_custom_call" | custom-call | tf_op jit(solution)/shard_map/mix_chunks/pallas_call | solution.py:324
  88.6 0.0 copy-done.3
  88.6 3.7 %convolution_convert_fusion = bf16[512,2048]{1,0:T(8,128)(2,1)} fusion(bf16[512,1024]{1,0:T(8,128)(2,1)S(1)} %mix_chunks.1, bf16[1024,2048]{1,0:T(8,128)(2,1)S(1)} %copy-done.3), kind=kOutput, calls=%fused_computation.2 | convolution fusion | flops 2148532224 | bytes 7340032 | tf_op jit(solution)/shard_map/dot_general | solution.py:333
  92.3 0.0 reduce-scatter.2.cloned.1.call-update
  92.3 8.9 %reduce-scatter.2.cloned.1.call-done = bf16[512,1024]{1,0:T(8,128)(2,1)} async-done(((bf16[512,2048]{1,0:T(8,128)(2,1)}), bf16[512,1024]{1,0:T(8,128)(2,1)}) %reduce-scatter.2.cloned.1.call-update) | async-done | bytes 1048592 | tf_op jit(solution)/shard_map/reduce_scatter | solution.py:334
Async XLA Ops:
  6.5 15.7 %copy-start = (bf16[2,2048,16]{1,2,0:T(8,128)(2,1)S(1)}, bf16[2,2048,16]{1,2,0:T(8,128)(2,1)}, u32[]{:S(2)}) copy-start(bf16[2,2048,16]{1,2,0:T(8,128)(2,1)} %param.11) | copy-start | bytes 393220
  6.5 18.2 %copy-start.2 = (f32[2,16]{1,0:T(2,128)S(1)}, f32[2,16]{1,0:T(2,128)}, u32[]{:S(2)}) copy-start(f32[2,16]{1,0:T(2,128)} %param.12) | copy-start | bytes 388
  6.5 15.7 %all-gather.3.cloned.1.call-start = ((), (), s32[]{:S(2)}) async-start(), calls=%async_computation.1 | async-start | bytes 3145728 | tf_op jit(solution)/shard_map/all_gather | solution.py:266
  7.3 26.7 %all-gather.5.cloned.1.call-start = ((), (), s32[]{:S(2)}) async-start(), calls=%async_computation.2 | async-start | bytes 1572864 | tf_op jit(solution)/shard_map/all_gather | solution.py:269
  8.0 93.2 %reduce-scatter.2.cloned.1.call-start = ((), (), s32[]{:S(2)}) async-start(), calls=%async_computation.3 | async-start | bytes 3145728 | tf_op jit(solution)/shard_map/reduce_scatter | solution.py:334
  22.3 11.7 %copy-start.1 = (bf16[512,2048]{1,0:T(8,128)(2,1)S(1)}, bf16[512,2048]{1,0:T(8,128)(2,1)}, u32[]{:S(2)}) copy-start(bf16[512,2048]{1,0:T(8,128)(2,1)} %all-gather.3.cloned.1.call-done) | copy-start | bytes 6291460
  77.7 10.9 %copy-start.3 = (bf16[1024,2048]{1,0:T(8,128)(2,1)S(1)}, bf16[1024,2048]{1,0:T(8,128)(2,1)}, u32[]{:S(2)}) copy-start(bf16[1024,2048]{1,0:T(8,128)(2,1)} %param.15) | copy-start | bytes 12582916
Sparse Core Ops, SparseCore 0:
  8.9 13.3 all-gather.2
  23.8 10.1 all-gather.4
  92.4 8.7 reduce-scatter.1

commit v2 on v1

--- a/solution.py
+++ b/solution.py
@@ -11,6 +11,7 @@
 STATE = 128
 CHUNK = 128
 GROUP = 4
+PARTS = 4
 VMEM_LIMIT = 48 * 1024 * 1024
 F32 = jnp.float32
 BF16 = jnp.bfloat16
@@ -42,6 +43,64 @@
     running = (rows >= cols).astype(F32)
     upto = dot(running, logs, precision=HIGH)
     return steps, upto, upto - logs
+
+
+def gather_kernel(n, tokens_ref, bc_ref, dt_ref, bias_ref, whole_ref, both_ref, raw_ref, columns, *sems):
+    send_bc, recv_bc, send_tok, recv_tok = sems
+    me = lax.axis_index("tp")
+    length, width = tokens_ref.shape
+
+    barrier = pltpu.get_barrier_semaphore()
+    for d in range(1, n):
+        pl.semaphore_signal(
+            barrier, inc=1, device_id={"tp": (me + d) % n}, device_id_type=pl.DeviceIdType.MESH
+        )
+    pl.semaphore_wait(barrier, n - 1)
+
+    def features(owner):
+        return pl.ds(pl.multiple_of(owner * width, width), width)
+
+    weights, parts = [], []
+    for d in range(1, n):
+        to = {"tp": (me + d) % n}
+        weights.append(
+            pltpu.make_async_remote_copy(
+                src_ref=bc_ref,
+                dst_ref=columns.at[me],
+                send_sem=send_bc.at[d - 1],
+                recv_sem=recv_bc.at[d - 1],
+                device_id=to,
+                device_id_type=pl.DeviceIdType.MESH,
+            )
+        )
+        parts.append(
+            pltpu.make_async_remote_copy(
+                src_ref=tokens_ref,
+                dst_ref=whole_ref.at[:, features(me)],
+                send_sem=send_tok.at[d - 1],
+                recv_sem=recv_tok.at[d - 1],
+                device_id=to,
+                device_id_type=pl.DeviceIdType.MESH,
+            )
+        )
+    for copy in weights + parts:
+        copy.start()
+    whole_ref[:, features(me)] = tokens_ref[...]
+    columns[me] = bc_ref[...]
+    for copy in weights:
+        copy.wait()
+    both = None
+    raw = bias_ref[...]
+    for d in range(n):
+        if d:
+            parts[d - 1].wait()
+        here = features((me + n - d) % n)
+        part = tokens_ref[...] if d == 0 else whole_ref[:, here]
+        new = jnp.concatenate([dot(part, columns[s, here, :]) for s in range(n)], axis=1)
+        both = new if both is None else both + new
+        raw = raw + dot(part, dt_ref[:, here], ((1,), (1,)))
+    both_ref[...] = both.astype(BF16)
+    raw_ref[...] = raw
 
 
 def states_kernel(proj_ref, both_ref, raw_ref, rate_ref, local_ref, send_ref, total_ref, sums):
@@ -128,58 +187,103 @@
         copy.start()
         return copy
 
-    copies = []
+    bands = [pl.ds(p * (STATE // PARTS), STATE // PARTS) for p in range(PARTS)]
+
+    first = [[] for _ in bands]
     for d in range(1, GROUP):
         to = (g + d) % GROUP
-        copies.append(push(total_ref.at[to], got_total.at[g], send1, recv1, 2 * d - 1, peer(z, to)))
-        copies.append(push(send_ref.at[to], got.at[g], send1, recv1, 2 * d - 2, peer(z, to)))
+        first[0].append(push(total_ref.at[to], got_total.at[g], send1, recv1, d - 1, peer(z, to)))
+    for p, band in enumerate(bands):
+        for d in range(1, GROUP):
+            to = (g + d) % GROUP
+            slot = (p + 1) * (GROUP - 1) + d - 1
+            source = send_ref.at[to, :, band, :]
+            first[p].append(push(source, got.at[g, :, band, :], send1, recv1, slot, peer(z, to)))
     got[g] = send_ref[g]
     got_total[g] = total_ref[g]
-    for copy in copies:
-        copy.wait()
-    before = [[None] * GROUP, [None] * GROUP]
-    for way in range(2):
-        order = range(GROUP) if way == 0 else range(GROUP - 1, -1, -1)
-        carry = jnp.zeros(got.shape[2:], F32)
-        passed = jnp.zeros(got_total.shape[2:], F32)
-        for s in order:
-            inner[s, way] = carry
-            before[way][s] = jnp.exp(passed[:1])
-            carry = jnp.exp(got_total[s, way][:1]) * carry + got[s, way].astype(F32)
-            passed = passed + got_total[s, way]
-        group[way] = carry.astype(BF16)
-        group_total[way] = passed
-
-    copies = []
-    for d in range(1, outer):
-        way = (z + d) // outer
-        to = peer((z + d) % outer, g)
-        copies.append(push(group_total.at[way], far_total.at[z], send2, recv2, 2 * d - 1, to))
-        copies.append(push(group.at[way], far.at[z], send2, recv2, 2 * d - 2, to))
     far[z] = jnp.zeros(far.shape[1:], BF16)
     far_total[z] = jnp.zeros(far_total.shape[1:], F32)
-    for copy in copies:
-        copy.wait()
-    for way in range(2):
-        order = range(outer) if way == 0 else range(outer - 1, -1, -1)
-        carry = jnp.zeros(far.shape[1:], F32)
-        for s in order:
-            longer = jnp.exp(far_total[s][:1]) * carry + far[s].astype(F32)
-            carry = jnp.where(s < z if way == 0 else s > z, longer, carry)
-        for s in range(GROUP):
-            back[s, way] = (inner[s, way] + before[way][s] * carry).astype(BF16)
-
-    copies = []
-    for d in range(1, GROUP):
-        to = (g + d) % GROUP
-        copies.append(push(back.at[to], landed.at[g], send3, recv3, d - 1, peer(z, to)))
+    before = [[None] * GROUP, [None] * GROUP]
+    second = [[] for _ in bands]
+    for p, band in enumerate(bands):
+        for copy in first[p]:
+            copy.wait()
+        for way in range(2):
+            order = range(GROUP) if way == 0 else range(GROUP - 1, -1, -1)
+            carry = jnp.zeros((STATE // PARTS, got.shape[3]), F32)
+            passed = jnp.zeros(got_total.shape[2:], F32)
+            for s in order:
+                inner[s, way, band, :] = carry
+                before[way][s] = jnp.exp(passed[:1])
+                carry = jnp.exp(got_total[s, way][:1]) * carry + got[s, way, band, :].astype(F32)
+                passed = passed + got_total[s, way]
+            group[way, band, :] = carry.astype(BF16)
+            if p == 0:
+                group_total[way] = passed
+
+        for d in range(1, outer):
+            way = (z + d) // outer
+            to = peer((z + d) % outer, g)
+            if p == 0:
+                total = group_total.at[way]
+                second[p].append(push(total, far_total.at[z], send2, recv2, d - 1, to))
+            slot = (p + 1) * (outer - 1) + d - 1
+            source = group.at[way, band, :]
+            second[p].append(push(source, far.at[z, band, :], send2, recv2, slot, to))
+
+    third = []
+    for p, band in enumerate(bands):
+        for copy in second[p]:
+            copy.wait()
+        for way in range(2):
+            order = range(outer) if way == 0 else range(outer - 1, -1, -1)
+            carry = jnp.zeros((STATE // PARTS, far.shape[2]), F32)
+            for s in order:
+                longer = jnp.exp(far_total[s][:1]) * carry + far[s, band, :].astype(F32)
+                carry = jnp.where(s < z if way == 0 else s > z, longer, carry)
+            for s in range(GROUP):
+                entering = inner[s, way, band, :] + before[way][s] * carry
+                back[s, way, band, :] = entering.astype(BF16)
+
+        for d in range(1, GROUP):
+            to = (g + d) % GROUP
+            slot = p * (GROUP - 1) + d - 1
+            source = back.at[to, :, band, :]
+            third.append(push(source, landed.at[g, :, band, :], send3, recv3, slot, peer(z, to)))
     landed[g] = back[g]
-    for copy in copies:
+    for copy in third:
         copy.wait()
     enter_ref[...] = landed[...]
 
 
-def mix_kernel(proj_ref, both_ref, raw_ref, rate_ref, gain_ref, local_ref, enter_ref, out_ref, wide):
+def mix_kernel(
+    n,
+    proj_ref,
+    both_ref,
+    raw_ref,
+    rate_ref,
+    gain_ref,
+    local_ref,
+    enter_ref,
+    weight_ref,
+    out_ref,
+    wide,
+    hidden,
+    own,
+    leaving,
+    arrived,
+    send,
+    recv,
+):
+    me = lax.axis_index("tp")
+    columns = out_ref.shape[1]
+    barrier = pltpu.get_barrier_semaphore()
+    for d in range(1, n):
+        pl.semaphore_signal(
+            barrier, inc=1, device_id={"tp": (me + d) % n}, device_id_type=pl.DeviceIdType.MESH
+        )
+    pl.semaphore_wait(barrier, n - 1)
+    copies = []
     heads2 = raw_ref.shape[1]
     heads = heads2 // 2
     width = heads * HEAD_DIM
@@ -255,7 +359,33 @@
         unit = spread_one[:heads]
         power = dot(high, unit, ((1,), (1,))) + dot(low, unit, ((1,), (1,)))
         norm = lax.rsqrt(power * (1.0 / HEAD_DIM) + 1e-05)
-        out_ref[rows, :] = (gated * dot(split_wide(norm), spread_one)).astype(BF16)
+        hidden[rows, :] = (gated * dot(split_wide(norm), spread_one)).astype(BF16)
+        if c % 2 == 0:
+            continue
+        rows = slice((c - 1) * CHUNK, (c + 1) * CHUNK)
+        for d in range(1, n):
+            to = (me + d) % n
+            theirs = pl.ds(pl.multiple_of(to * columns, columns), columns)
+            leaving[d - 1, rows, :] = dot(hidden[rows, :], weight_ref[:, theirs]).astype(BF16)
+            slot = c // 2 * (n - 1) + d - 1
+            copy = pltpu.make_async_remote_copy(
+                src_ref=leaving.at[d - 1, rows, :],
+                dst_ref=arrived.at[d - 1, rows, :],
+                send_sem=send.at[slot],
+                recv_sem=recv.at[slot],
+                device_id={"tp": to},
+                device_id_type=pl.DeviceIdType.MESH,
+            )
+            copy.start()
+            copies.append(copy)
+        mine = pl.ds(pl.multiple_of(me * columns, columns), columns)
+        own[rows, :] = dot(hidden[rows, :], weight_ref[:, mine]).astype(BF16)
+    for copy in copies:
+        copy.wait()
+    total = own[...].astype(F32)
+    for d in range(1, n):
+        total = total + arrived[d - 1].astype(F32)
+    out_ref[...] = total.astype(BF16)
 
 
 def shards(tokens, in_weight, bc_weight, dt_weight, dt_bias, decay_rate, skip_gain, out_weight):
@@ -263,18 +393,36 @@
     width = heads * HEAD_DIM
     quarter = width // GROUP
     outer = lax.axis_size("seq") // GROUP
-    whole = lax.all_gather(tokens, "tp", axis=1, tiled=True)
-    length = whole.shape[0]
+    n = lax.axis_size("tp")
+    length = tokens.shape[0]
+    features = dt_weight.shape[1]
     chunks = length // CHUNK
-    full_columns = lax.all_gather(bc_weight, "tp", axis=1, tiled=True)
+    params = pltpu.CompilerParams(vmem_limit_bytes=VMEM_LIMIT)
+    vmem = pl.BlockSpec(memory_space=pltpu.VMEM)
+    whole, both, raw = pl.pallas_call(
+        functools.partial(gather_kernel, n),
+        out_shape=(
+            jax.ShapeDtypeStruct((length, features), BF16),
+            jax.ShapeDtypeStruct((length, 2 * STATE), BF16),
+            jax.ShapeDtypeStruct((length, 2 * heads), F32),
+        ),
+        in_specs=[vmem] * 4,
+        out_specs=(vmem, vmem, vmem),
+        scratch_shapes=[pltpu.VMEM((n,) + bc_weight.shape, BF16)]
+        + [pltpu.SemaphoreType.DMA((n - 1,))] * 4,
+        compiler_params=pltpu.CompilerParams(
+            vmem_limit_bytes=VMEM_LIMIT, collective_id=1, has_side_effects=True
+        ),
+        name="gather_features",
+    )(
+        tokens,
+        bc_weight,
+        dt_weight.transpose(0, 2, 1).reshape(2 * heads, features),
+        dt_bias.reshape(1, 2 * heads),
+    )
     projected = jnp.einsum("td,dkf->ktf", whole, in_weight, preferred_element_type=F32)
-    both = jnp.dot(whole, full_columns, preferred_element_type=F32).astype(BF16)
-    raw = jnp.einsum("td,kdh->tkh", whole, dt_weight, preferred_element_type=F32)
-    raw = (raw + dt_bias[None]).reshape(length, 2 * heads)
     rate = jnp.concatenate([decay_rate, decay_rate])[None, :]
     gain = jnp.repeat(skip_gain, HEAD_DIM)[None, :]
-    params = pltpu.CompilerParams(vmem_limit_bytes=VMEM_LIMIT)
-    vmem = pl.BlockSpec(memory_space=pltpu.VMEM)
     local, send, total = pl.pallas_call(
         states_kernel,
         out_shape=(
@@ -309,29 +457,38 @@
             pltpu.VMEM((outer, 8, quarter), F32),
             pltpu.VMEM((GROUP, 2, STATE, quarter), BF16),
             pltpu.VMEM((GROUP, 2, STATE, quarter), BF16),
-            pltpu.SemaphoreType.DMA((2 * GROUP - 2,)),
-            pltpu.SemaphoreType.DMA((2 * GROUP - 2,)),
-            pltpu.SemaphoreType.DMA((2 * outer - 2,)),
-            pltpu.SemaphoreType.DMA((2 * outer - 2,)),
-            pltpu.SemaphoreType.DMA((GROUP - 1,)),
-            pltpu.SemaphoreType.DMA((GROUP - 1,)),
+            pltpu.SemaphoreType.DMA(((PARTS + 1) * (GROUP - 1),)),
+            pltpu.SemaphoreType.DMA(((PARTS + 1) * (GROUP - 1),)),
+            pltpu.SemaphoreType.DMA(((PARTS + 1) * (outer - 1),)),
+            pltpu.SemaphoreType.DMA(((PARTS + 1) * (outer - 1),)),
+            pltpu.SemaphoreType.DMA((PARTS * (GROUP - 1),)),
+            pltpu.SemaphoreType.DMA((PARTS * (GROUP - 1),)),
         ],
         compiler_params=pltpu.CompilerParams(
             vmem_limit_bytes=VMEM_LIMIT, collective_id=0, has_side_effects=True
         ),
         name="carry_states",
     )(send, total)
-    hidden = pl.pallas_call(
-        mix_kernel,
-        out_shape=jax.ShapeDtypeStruct((length, width), BF16),
-        in_specs=[vmem] * 7,
+    columns = out_weight.shape[1] // n
+    return pl.pallas_call(
+        functools.partial(mix_kernel, n),
+        out_shape=jax.ShapeDtypeStruct((length, columns), BF16),
+        in_specs=[vmem] * 8,
         out_specs=vmem,
-        scratch_shapes=[pltpu.VMEM((STATE, 2 * width), F32)],
-        compiler_params=params,
+        scratch_shapes=[
+            pltpu.VMEM((STATE, 2 * width), F32),
+            pltpu.VMEM((length, width), BF16),
+            pltpu.VMEM((length, columns), BF16),
+            pltpu.VMEM((n - 1, length, columns), BF16),
+            pltpu.VMEM((n - 1, length, columns), BF16),
+            pltpu.SemaphoreType.DMA((chunks // 2 * (n - 1),)),
+            pltpu.SemaphoreType.DMA((chunks // 2 * (n - 1),)),
+        ],
+        compiler_params=pltpu.CompilerParams(
+            vmem_limit_bytes=VMEM_LIMIT, collective_id=2, has_side_effects=True
+        ),
         name="mix_chunks",
-    )(projected, both, raw, rate, gain, local, enter)
-    partial_terms = jnp.dot(hidden, out_weight, preferred_element_type=F32)
-    return lax.psum_scatter(partial_terms.astype(BF16), "tp", scatter_dimension=1, tiled=True)
+    )(projected, both, raw, rate, gain, local, enter, out_weight)
 
 
 def solution(mesh):

time: 108 us -> 65.2 us (0.60)
  waiting for transfers between devices: 32 us -> 0 us
  between operations: 13.2 us -> 0.04 us
  matrix products: 18.6 us -> 10.5 us
  Pallas kernels: 42.1 us -> 47.8 us
  local copies, waits for them, and re-layouts: 0.96 us -> 5.71 us
    all_gather x2 -> x0, waiting for transfers between devices: 21.6 us -> none  [the longest x1 12.6 us: shards(): whole = lax.all_gather(tokens, 'tp', axis=1, tiled=True)]
    pallas_call x1 -> x2, Pallas kernels: 10.9 us -> 20.5 us  [the longest x1 15.7 us: shards(): pl.pallas_call(functools.partial(mix_kernel, n), out_shape=jax.ShapeDtype...]
    reduce_scatter x1 -> x0, waiting for transfers between devices: 8.9 us -> none  [shards(): lax.psum_scatter(partial_terms.astype(BF16), 'tp', scatter_dimension=1, t...]
    dot_general x2 -> x0, matrix products: 5.6 us -> none  [the longest x1 3.67 us: shards(): partial_terms = jnp.dot(hidden, out_weight, preferred_element_type=F32)]
    unnamed x8 -> x7, local copies, waits for them, and re-layouts: 0.03 us -> 4.14 us
    pallas_call x1, Pallas kernels: 25.9 us -> 22 us  [shards(): pl.pallas_call(functools.partial(carry_kernel, outer), out_shape=jax.Shap...]
    unnamed x1 -> x0, matrix products: 2.46 us -> none
    unnamed x3 -> x0, waiting for transfers between devices: 1.42 us -> none
  transfers between devices with their start and end apart: 3 -> 0, of which waited for: 3 -> 0; matrix products, arithmetic and copies ran while one was open for 4% -> 0% of each run, Pallas kernels for 0% -> 0%
where the time goes in v2:
time: 65.2 us; the launch traced here: 64.9 us
  Pallas kernels  47.8 us (73%)
  matrix products  10.5 us (16%)
  local copies, waits for them, and re-layouts  5.71 us (9%)
  other arithmetic  0.8 us (1%)
    pallas_call x1, Pallas kernels, shards(): pl.pallas_call(functools.partial(carry_kernel, outer), out_shape=jax.Shap...  22 us
    pallas_call x1, Pallas kernels, shards(): pl.pallas_call(functools.partial(mix_kernel, n), out_shape=jax.ShapeDtype...  15.7 us
    dot_general x1, matrix products, shards(): jnp.einsum('td,dkf->ktf', whole, in_weight, preferred_element_type=F32)  10.5 us
    pallas_call x1, Pallas kernels, shards(): pl.pallas_call(states_kernel, out_shape=(jax.ShapeDtypeStruct((chunks, ST...  5.28 us
    pallas_call x1, Pallas kernels, shards(): pl.pallas_call(functools.partial(gather_kernel, n), out_shape=(jax.ShapeD...  4.79 us
    unnamed x7, local copies, waits for them, and re-layouts  4.14 us

profile of v2, /device:TPU:0, one launch (start us, length us, event | category | flops | bytes accessed | tf_op | source)
XLA Modules:
  0.0 64.9 jit_solution(4944710223244679589)
XLA Ops:
  0.0 0.8 %maximum_bitcast_fusion.rate_ref = f32[1,32]{1,0:T(1,128)S(1)} fusion(f32[16]{0:T(128)} %param.13), kind=kLoop, calls=%fused_computation.4 | loop fusion | flops 32 | bytes 192 | tf_op jit(solution)/shard_map/broadcast_in_dim | solution.py:424
  0.8 0.8 %reshape.7.bias_ref = f32[1,32]{1,0:T(1,128)S(1)} reshape(f32[2,16]{1,0:T(2,128)} %param.12) | data formatting | bytes 256 | tf_op jit(solution)/shard_map/reshape | solution.py:421
  1.6 0.7 %broadcast_in_dim.7 = f32[16,64]{1,0:T(8,128)S(1)} broadcast(f32[16]{0:T(128)} %param.14), dimensions={0} | broadcast | bytes 4160 | tf_op jit(solution)/shard_map/broadcast_in_dim | solution.py:425
  2.3 0.1 broadcast_in_dim_reshape.3.gain_ref
  2.4 0.0 copy-start
  2.4 1.2 %copy-done = bf16[512,1024]{1,0:T(8,128)(2,1)S(1)} copy-done((bf16[512,1024]{1,0:T(8,128)(2,1)S(1)}, bf16[512,1024]{1,0:T(8,128)(2,1)}, u32[]{:S(2)}) %copy-start) | copy-done | bytes 1048600
  3.6 0.0 copy-start.1
  3.6 1.0 %copy-done.1 = bf16[2048,128]{1,0:T(8,128)(2,1)S(1)} copy-done((bf16[2048,128]{1,0:T(8,128)(2,1)S(1)}, bf16[2048,128]{1,0:T(8,128)(2,1)}, u32[]{:S(2)}) %copy-start.1) | copy-done | bytes 524312
  4.6 0.0 copy-start.2
  4.6 0.9 %copy-done.2 = bf16[2,2048,16]{1,2,0:T(8,128)(2,1)S(1)} copy-done((bf16[2,2048,16]{1,2,0:T(8,128)(2,1)S(1)}, bf16[2,2048,16]{1,2,0:T(8,128)(2,1)}, u32[]{:S(2)}) %copy-start.2) | copy-done | bytes 131096
  5.5 4.8 %gather_features.1 = (bf16[512,2048]{1,0:T(8,128)(2,1)S(1)}, bf16[512,256]{1,0:T(8,128)(2,1)S(1)}, f32[512,32]{1,0:T(8,128)S(1)}) custom-call(bf16[512,1024]{1,0:T(8,128)(2,1)S(1)} %copy-done, bf16[2048,128]{1,0:T(8,128)(2,1)S(1)} %copy-done.1, bf16[32,2048]{1,0:T(8,128)(2,1)S(1)} %bitcast.10, f32[1,32]{1,0:T(1,128)S(1)} %reshape.7.bias_ref), custom_call_target="tpu_custom_call" | custom-call | tf_op jit(solution)/shard_map/gather_features/pallas_call | solution.py:402
  10.3 10.5 %fusion.2.proj_ref = f32[2,512,1024]{2,1,0:T(8,128)} fusion(bf16[2048,2,1024]{2,1,0:T(2,128)(2,1)} %param.9, bf16[512,2048]{1,0:T(8,128)(2,1)S(1)} %get-tuple-element.11), kind=kOutput, calls=%fused_computation.2 | convolution fusion | flops 4294967296 | bytes 14680064 | tf_op jit(solution)/shard_map/td,dkf->ktf/dot_general | solution.py:423
  20.9 5.3 %block_states.1 = (bf16[4,128,2048]{2,1,0:T(8,128)(2,1)S(1)}, bf16[4,2,128,256]{3,2,1,0:T(8,128)(2,1)S(1)}, f32[4,2,8,256]{3,2,1,0:T(8,128)S(1)}) custom-call(f32[2,512,1024]{2,1,0:T(8,128)} %fusion.2.proj_ref, bf16[512,256]{1,0:T(8,128)(2,1)S(1)} %get-tuple-element.12.both_ref, f32[512,32]{1,0:T(8,128)S(1)} %get-tuple-element.13.raw_ref, ...), custom_call_target="tpu_custom_call" | custom-call | tf_op jit(solution)/shard_map/block_states/pallas_call | solution.py:426
  26.2 22.0 %carry_states.1.enter_ref = bf16[4,2,128,256]{3,2,1,0:T(8,128)(2,1)S(1)} custom-call(bf16[4,2,128,256]{3,2,1,0:T(8,128)(2,1)S(1)} %get-tuple-element.15.send_ref, f32[4,2,8,256]{3,2,1,0:T(8,128)S(1)} %get-tuple-element.16.total_ref), custom_call_target="tpu_custom_call" | custom-call | tf_op jit(solution)/shard_map/carry_states/pallas_call | solution.py:445
  48.2 15.7 %mix_chunks.1 = bf16[512,1024]{1,0:T(8,128)(2,1)S(1)} custom-call(f32[2,512,1024]{2,1,0:T(8,128)} %fusion.2.proj_ref, bf16[512,256]{1,0:T(8,128)(2,1)S(1)} %get-tuple-element.12.both_ref, f32[512,32]{1,0:T(8,128)S(1)} %get-tuple-element.13.raw_ref, f32[1,32]{1,0:T(1,128)S(1)} %maximum_bitcast_fusion.rate_ref, ...), custom_call_target="tpu_custom_call" | custom-call | tf_op jit(solution)/shard_map/mix_chunks/pallas_call | solution.py:473
  63.9 1.0 %copy.15 = bf16[512,1024]{1,0:T(8,128)(2,1)} copy(bf16[512,1024]{1,0:T(8,128)(2,1)S(1)} %mix_chunks.1) | data formatting | bytes 2097152
Async XLA Ops:
  2.4 1.2 %copy-start = (bf16[512,1024]{1,0:T(8,128)(2,1)S(1)}, bf16[512,1024]{1,0:T(8,128)(2,1)}, u32[]{:S(2)}) copy-start(bf16[512,1024]{1,0:T(8,128)(2,1)} %tokens_ref.1) | copy-start | bytes 3145732
  3.6 1.0 %copy-start.1 = (bf16[2048,128]{1,0:T(8,128)(2,1)S(1)}, bf16[2048,128]{1,0:T(8,128)(2,1)}, u32[]{:S(2)}) copy-start(bf16[2048,128]{1,0:T(8,128)(2,1)} %bc_ref.1) | copy-start | bytes 1572868
  4.6 0.9 %copy-start.2 = (bf16[2,2048,16]{1,2,0:T(8,128)(2,1)S(1)}, bf16[2,2048,16]{1,2,0:T(8,128)(2,1)}, u32[]{:S(2)}) copy-start(bf16[2,2048,16]{1,2,0:T(8,128)(2,1)} %param.11) | copy-start | bytes 393220

commit v3 on v2

v3 whole, which is shorter than its diff:
```python
import functools

import jax
import jax.numpy as jnp
from jax import lax
from jax.experimental import pallas as pl
from jax.experimental.pallas import tpu as pltpu
from jax.sharding import PartitionSpec as P

HEAD_DIM = 64
STATE = 128
CHUNK = 128
GROUP = 4
PARTS = 4
VMEM_LIMIT = 48 * 1024 * 1024
F32 = jnp.float32
BF16 = jnp.bfloat16
HIGH = lax.Precision.HIGHEST


def dot(a, b, contract=((1,), (0,)), precision=None):
    return lax.dot_general(
        a, b, (contract, ((), ())), precision=precision, preferred_element_type=F32
    )


def split_wide(value):
    high = value.astype(BF16)
    return jnp.concatenate([high, (value - high.astype(F32)).astype(BF16)], axis=1)


def spread_matrix(count, dtype, copies=1):
    rows = lax.broadcasted_iota(jnp.int32, (copies * count, count * HEAD_DIM), 0)
    lanes = lax.broadcasted_iota(jnp.int32, (copies * count, count * HEAD_DIM), 1)
    return (lax.rem(rows, count) == lanes // HEAD_DIM).astype(dtype)


def gather_kernel(n, tokens_ref, bc_ref, dt_ref, bias_ref, whole_ref, both_ref, raw_ref, *scratch):
    columns, dt, send_bc, recv_bc, send_tok, recv_tok, here_sem = scratch
    me = lax.axis_index("tp")
    width = tokens_ref.shape[1]

    def features(owner):
        return pl.ds(pl.multiple_of(owner * width, width), width)

    own_bc = pltpu.make_async_copy(bc_ref, columns.at[me], here_sem.at[0])
    own_tokens = pltpu.make_async_copy(tokens_ref, whole_ref.at[:, features(me)], here_sem.at[1])
    own_dt = pltpu.make_async_copy(dt_ref, dt, here_sem.at[2])
    barrier = pltpu.get_barrier_semaphore()
    for d in range(1, n):
        pl.semaphore_signal(
            barrier, inc=1, device_id={"tp": (me + d) % n}, device_id_type=pl.DeviceIdType.MESH
        )
    own_bc.start()
    own_tokens.start()
    own_dt.start()
    pl.semaphore_wait(barrier, n - 1)
    weights, parts = [], []
    for d in range(1, n):
        to = {"tp": (me + d) % n}
        weights.append(
            pltpu.make_async_remote_copy(
                src_ref=bc_ref,
                dst_ref=columns.at[me],
                send_sem=send_bc.at[d - 1],
                recv_sem=recv_bc.at[d - 1],
                device_id=to,
                device_id_type=pl.DeviceIdType.MESH,
            )
        )
        parts.append(
            pltpu.make_async_remote_copy(
                src_ref=tokens_ref,
                dst_ref=whole_ref.at[:, features(me)],
                send_sem=send_tok.at[d - 1],
                recv_sem=recv_tok.at[d - 1],
                device_id=to,
                device_id_type=pl.DeviceIdType.MESH,
            )
        )
    for copy in weights + parts:
        copy.start()
    own_bc.wait()
    own_tokens.wait()
    own_dt.wait()
    for copy in weights:
        copy.wait()
    both = None
    raw = jnp.concatenate([bias_ref[:1, :], bias_ref[1:, :]], axis=1)
    for d in range(n):
        if d:
            parts[d - 1].wait()
        here = features((me + n - d) % n)
        part = whole_ref[:, here]
        new = jnp.concatenate([dot(part, columns[s, here, :]) for s in range(n)], axis=1)
        both = new if both is None else both + new
        raw = raw + dot(part, dt[:, here], ((1,), (1,)))
    both_ref[...] = both.astype(BF16)
    raw_ref[...] = raw


def mixer_kernel(
    outer,
    n,
    proj_ref,
    both_ref,
    raw_ref,
    rate_ref,
    gain_ref,
    weight_hbm,
    out_ref,
    values_wide,
    gates,
    weight_ref,
    sums,
    local,
    mix,
    send_ref,
    total_ref,
    got,
    got_total,
    inner,
    group,
    group_total,
    far,
    far_total,
    back,
    landed,
    hidden,
    own,
    leaving,
    arrived,
    send1,
    recv1,
    send2,
    recv2,
    send3,
    recv3,
    send4,
    recv4,
    here_sem,
):
    seq = lax.axis_index("seq")
    me = lax.axis_index("tp")
    z, g = seq // GROUP, seq % GROUP
    heads2 = raw_ref.shape[1]
    heads = heads2 // 2
    width = heads * HEAD_DIM
    chunks = raw_ref.shape[0] // CHUNK
    quarter = width // GROUP
    columns = out_ref.shape[1]

    get_values = pltpu.make_async_copy(proj_ref.at[0], values_wide, here_sem.at[0])
    get_gates = pltpu.make_async_copy(proj_ref.at[1], gates, here_sem.at[1])
    get_weight = pltpu.make_async_copy(weight_hbm, weight_ref, here_sem.at[2])
    get_values.start()
    get_gates.start()
    get_weight.start()

    def peer(zz, gg):
        return {"seq": zz * GROUP + gg}

    barrier = pltpu.get_barrier_semaphore()
    friends = [peer(z, (g + d) % GROUP) for d in range(1, GROUP)]
    friends += [peer((z + d) % outer, g) for d in range(1, outer)]
    friends += [{"tp": (me + d) % n} for d in range(1, n)]
    for friend in friends:
        pl.semaphore_signal(barrier, inc=1, device_id=friend, device_id_type=pl.DeviceIdType.MESH)

    def push(source, target, sends, recvs, slot, where):
        copy = pltpu.make_async_remote_copy(
            src_ref=source,
            dst_ref=target,
            send_sem=sends.at[slot],
            recv_sem=recvs.at[slot],
            device_id=where,
            device_id_type=pl.DeviceIdType.MESH,
        )
        copy.start()
        return copy

    every = chunks * heads2
    raw = jnp.concatenate(
        [raw_ref[c * CHUNK : (c + 1) * CHUNK, :] for c in range(chunks)], axis=1
    )
    rate = jnp.concatenate([rate_ref[...]] * (2 * chunks), axis=1)
    steps = jnp.maximum(raw, 0.0) + jnp.log1p(jnp.exp(-jnp.abs(raw)))
    logs = -rate * steps
    rows_of = lax.broadcasted_iota(jnp.int32, (CHUNK, CHUNK), 0)
    cols_of = lax.broadcasted_iota(jnp.int32, (CHUNK, CHUNK), 1)
    upto = dot((rows_of >= cols_of).astype(F32), logs, precision=HIGH)
    before = upto - logs
    last = upto[CHUNK - 1 : CHUNK, :]
    forward = lax.rem(lax.broadcasted_iota(jnp.int32, (CHUNK, every), 1), heads2) < heads
    weight = jnp.exp(jnp.where(forward, last - upto, before)) * steps
    column = jnp.where(forward, before, -upto)
    row = (jnp.where(forward, -upto, before) + jnp.log(steps)).T
    scale = jnp.exp(jnp.where(forward, before, last - upto))
    lasts = [last[:, c * heads2 : (c + 1) * heads2] for c in range(chunks)]
    passed = []
    for c in range(chunks):
        gone = jnp.zeros((1, heads2), F32)
        for other in range(chunks):
            if other < c:
                gone = gone + jnp.where(forward[:1, :heads2], lasts[other], 0.0)
            if other > c:
                gone = gone + jnp.where(forward[:1, :heads2], 0.0, lasts[other])
        passed.append(gone)
    enter_scale = scale * jnp.exp(jnp.concatenate(passed, axis=1))
    spread = spread_matrix(heads2, BF16, 2)
    spread_one = spread_matrix(heads, BF16, 2)
    stack = lasts + [functools.reduce(jnp.add, lasts)]
    stack = stack + [jnp.zeros((1, heads2), F32)] * (8 - len(stack))
    totals = dot(jnp.concatenate(stack, axis=0), spread_matrix(heads2, F32), precision=HIGH)
    gain = jnp.broadcast_to(gain_ref[...], (8, heads))
    gain = dot(gain, spread_matrix(heads, F32), precision=HIGH)[:1]

    def spread_chunk(value, c):
        return dot(split_wide(value[:, c * heads2 : (c + 1) * heads2]), spread)

    get_values.wait()
    for c in range(chunks):
        rows = slice(c * CHUNK, (c + 1) * CHUNK)
        values = values_wide[rows, :].astype(BF16).astype(F32)
        weighted = jnp.concatenate([values, values], axis=1) * spread_chunk(weight, c)
        sums[c] = dot(both_ref[rows, :STATE], weighted.astype(BF16), ((0,), (0,)))
    for way in range(2):
        side = slice(way * width, (way + 1) * width)
        carry = jnp.zeros((STATE, width), F32)
        for c in range(chunks) if way == 0 else range(chunks - 1, -1, -1):
            local[c, :, side] = carry.astype(BF16)
            carry = jnp.exp(totals[c : c + 1, side]) * carry + sums[c, :, side]
        for q in range(GROUP):
            part = slice(q * quarter, (q + 1) * quarter)
            send_ref[q, way] = carry[:, part].astype(BF16)
            total = totals[chunks : chunks + 1, side][:, part]
            total_ref[q, way] = jnp.broadcast_to(total, (8, quarter))

    pl.semaphore_wait(barrier, GROUP - 1 + outer - 1 + n - 1)

    bands = [pl.ds(p * (STATE // PARTS), STATE // PARTS) for p in range(PARTS)]

    first = [[] for _ in bands]
    for d in range(1, GROUP):
        to = (g + d) % GROUP
        first[0].append(push(total_ref.at[to], got_total.at[g], send1, recv1, d - 1, peer(z, to)))
    for p, band in enumerate(bands):
        for d in range(1, GROUP):
            to = (g + d) % GROUP
            slot = (p + 1) * (GROUP - 1) + d - 1
            source = send_ref.at[to, :, band, :]
            first[p].append(push(source, got.at[g, :, band, :], send1, recv1, slot, peer(z, to)))
    got[g] = send_ref[g]
    got_total[g] = total_ref[g]
    far[z] = jnp.zeros(far.shape[1:], BF16)
    far_total[z] = jnp.zeros(far_total.shape[1:], F32)

    lower = rows_of > cols_of
    on_line = rows_of == cols_of
    first_half = lax.broadcasted_iota(jnp.int32, (CHUNK, 2 * HEAD_DIM), 1) < HEAD_DIM

    def inside(c):
        rows = slice(c * CHUNK, (c + 1) * CHUNK)
        scores = dot(both_ref[rows, STATE:], both_ref[rows, :STATE], ((1,), (1,)))
        for pair in range(heads // 2):
            weights = []
            for h in (2 * pair, 2 * pair + 1):
                f = c * heads2 + h
                b = f + heads
                power = jnp.where(
                    lower,
                    column[:, f : f + 1] + row[f : f + 1, :],
                    column[:, b : b + 1] + row[b : b + 1, :],
                )
                power = jnp.where(on_line, -jnp.inf, power)
                weights.append((scores * jnp.exp(power)).astype(BF16))
            lanes = slice(pair * 2 * HEAD_DIM, (pair + 1) * 2 * HEAD_DIM)
            pair_values = values_wide[rows, lanes].astype(BF16)
            zero = jnp.zeros_like(pair_values)
            stacked = jnp.concatenate(
                [
                    jnp.where(first_half, pair_values, zero),
                    jnp.where(first_half, zero, pair_values),
                ],
                axis=0,
            )
            mix[rows, lanes] = dot(jnp.concatenate(weights, axis=1), stacked)

    def nearby(c):
        rows = slice(c * CHUNK, (c + 1) * CHUNK)
        reach = dot(both_ref[rows, STATE:], local[c]) * spread_chunk(scale, c)
        values = values_wide[rows, :].astype(BF16).astype(F32)
        mix[rows, :] = mix[rows, :] + reach[:, :width] + reach[:, width:] + gain * values

    inside(0)
    if chunks > 1:
        inside(1)
    before_state = [[None] * GROUP, [None] * GROUP]
    second = [[] for _ in bands]
    for p, band in enumerate(bands):
        for copy in first[p]:
            copy.wait()
        for way in range(2):
            carry = jnp.zeros((STATE // PARTS, quarter), F32)
            gone = jnp.zeros((8, quarter), F32)
            for s in range(GROUP) if way == 0 else range(GROUP - 1, -1, -1):
                inner[s, way, band, :] = carry
                before_state[way][s] = jnp.exp(gone[:1])
                carry = jnp.exp(got_total[s, way][:1]) * carry + got[s, way, band, :].astype(F32)
                gone = gone + got_total[s, way]
            group[way, band, :] = carry.astype(BF16)
            if p == 0:
                group_total[way] = gone

        for d in range(1, outer):
            way = (z + d) // outer
            to = peer((z + d) % outer, g)
            if p == 0:
                total = group_total.at[way]
                second[p].append(push(total, far_total.at[z], send2, recv2, d - 1, to))
            slot = (p + 1) * (outer - 1) + d - 1
            source = group.at[way, band, :]
            second[p].append(push(source, far.at[z, band, :], send2, recv2, slot, to))

    for c in range(2, chunks):
        inside(c)
    third = []
    for p, band in enumerate(bands):
        for copy in second[p]:
            copy.wait()
        for way in range(2):
            carry = jnp.zeros((STATE // PARTS, quarter), F32)
            for s in range(outer) if way == 0 else range(outer - 1, -1, -1):
                longer = jnp.exp(far_total[s][:1]) * carry + far[s, band, :].astype(F32)
                carry = jnp.where(s < z if way == 0 else s > z, longer, carry)
            for s in range(GROUP):
                entering = inner[s, way, band, :] + before_state[way][s] * carry
                back[s, way, band, :] = entering.astype(BF16)

        for d in range(1, GROUP):
            to = (g + d) % GROUP
            slot = p * (GROUP - 1) + d - 1
            source = back.at[to, :, band, :]
            third.append(push(source, landed.at[g, :, band, :], send3, recv3, slot, peer(z, to)))
    landed[g] = back[g]
    get_gates.wait()
    for c in range(chunks):
        nearby(c)
        rows = slice(c * CHUNK, (c + 1) * CHUNK)
        gates[rows, :] = gates[rows, :] / (1.0 + jnp.exp(-gates[rows, :]))
    get_weight.wait()
    for copy in third:
        copy.wait()

    copies = []
    for c in range(chunks):
        rows = slice(c * CHUNK, (c + 1) * CHUNK)
        queries = both_ref[rows, STATE:]
        reach = [dot(queries, landed[q, way]) for way in range(2) for q in range(GROUP)]
        reach = jnp.concatenate(reach, axis=1) * spread_chunk(enter_scale, c)
        gated = (mix[rows, :] + reach[:, :width] + reach[:, width:]) * gates[rows, :]
        square = gated * gated
        high = square.astype(BF16)
        low = (square - high.astype(F32)).astype(BF16)
        unit = spread_one[:heads]
        power = dot(high, unit, ((1,), (1,))) + dot(low, unit, ((1,), (1,)))
        norm = lax.rsqrt(power * (1.0 / HEAD_DIM) + 1e-05)
        hidden[rows, :] = (gated * dot(split_wide(norm), spread_one)).astype(BF16)
        if c % 2 == 0:
            continue
        rows = slice((c - 1) * CHUNK, (c + 1) * CHUNK)
        for d in range(1, n):
            to = (me + d) % n
            theirs = pl.ds(pl.multiple_of(to * columns, columns), columns)
            leaving[d - 1, rows, :] = dot(hidden[rows, :], weight_ref[:, theirs]).astype(BF16)
            slot = c // 2 * (n - 1) + d - 1
            source = leaving.at[d - 1, rows, :]
            copies.append(
                push(source, arrived.at[d - 1, rows, :], send4, recv4, slot, {"tp": to})
            )
        mine = pl.ds(pl.multiple_of(me * columns, columns), columns)
        own[rows, :] = dot(hidden[rows, :], weight_ref[:, mine]).astype(BF16)
    for copy in copies:
        copy.wait()
    total = own[...].astype(F32)
    for d in range(1, n):
        total = total + arrived[d - 1].astype(F32)
    out_ref[...] = total.astype(BF16)


def shards(tokens, in_weight, bc_weight, dt_weight, dt_bias, decay_rate, skip_gain, out_weight):
    heads = decay_rate.shape[0]
    width = heads * HEAD_DIM
    quarter = width // GROUP
    outer = lax.axis_size("seq") // GROUP
    n = lax.axis_size("tp")
    length = tokens.shape[0]
    features = dt_weight.shape[1]
    chunks = length // CHUNK
    columns = out_weight.shape[1] // n
    vmem = pl.BlockSpec(memory_space=pltpu.VMEM)
    anywhere = pl.BlockSpec(memory_space=pl.ANY)
    dma = pltpu.SemaphoreType.DMA
    whole, both, raw = pl.pallas_call(
        functools.partial(gather_kernel, n),
        out_shape=(
            jax.ShapeDtypeStruct((length, features), BF16),
            jax.ShapeDtypeStruct((length, 2 * STATE), BF16),
            jax.ShapeDtypeStruct((length, 2 * heads), F32),
        ),
        in_specs=[pl.BlockSpec(memory_space=pltpu.HBM)] * 3 + [vmem],
        out_specs=(vmem, vmem, vmem),
        scratch_shapes=[
            pltpu.VMEM((n,) + bc_weight.shape, BF16),
            pltpu.VMEM((2 * heads, features), BF16),
        ]
        + [dma((n - 1,))] * 4
        + [dma((3,))],
        compiler_params=pltpu.CompilerParams(
            vmem_limit_bytes=VMEM_LIMIT, collective_id=0, has_side_effects=True
        ),
        name="gather_features",
    )(
        tokens,
        bc_weight,
        dt_weight.transpose(0, 2, 1).reshape(2 * heads, features),
        dt_bias,
    )
    projected = jnp.einsum("td,dkf->ktf", whole, in_weight, preferred_element_type=F32)
    return pl.pallas_call(
        functools.partial(mixer_kernel, outer, n),
        out_shape=jax.ShapeDtypeStruct((length, columns), BF16),
        in_specs=[anywhere, vmem, vmem, vmem, vmem, anywhere],
        out_specs=vmem,
        scratch_shapes=[
            pltpu.VMEM((length, width), F32),
            pltpu.VMEM((length, width), F32),
            pltpu.VMEM(out_weight.shape, BF16),
            pltpu.VMEM((chunks, STATE, 2 * width), F32),
            pltpu.VMEM((chunks, STATE, 2 * width), BF16),
            pltpu.VMEM((length, width), F32),
            pltpu.VMEM((GROUP, 2, STATE, quarter), BF16),
            pltpu.VMEM((GROUP, 2, 8, quarter), F32),
            pltpu.VMEM((GROUP, 2, STATE, quarter), BF16),
            pltpu.VMEM((GROUP, 2, 8, quarter), F32),
            pltpu.VMEM((GROUP, 2, STATE, quarter), F32),
            pltpu.VMEM((2, STATE, quarter), BF16),
            pltpu.VMEM((2, 8, quarter), F32),
            pltpu.VMEM((outer, STATE, quarter), BF16),
            pltpu.VMEM((outer, 8, quarter), F32),
            pltpu.VMEM((GROUP, 2, STATE, quarter), BF16),
            pltpu.VMEM((GROUP, 2, STATE, quarter), BF16),
            pltpu.VMEM((length, width), BF16),
            pltpu.VMEM((length, columns), BF16),
            pltpu.VMEM((n - 1, length, columns), BF16),
            pltpu.VMEM((n - 1, length, columns), BF16),
        ]
        + [dma(((PARTS + 1) * (GROUP - 1),))] * 2
        + [dma(((PARTS + 1) * (outer - 1),))] * 2
        + [dma((PARTS * (GROUP - 1),))] * 2
        + [dma((chunks // 2 * (n - 1),))] * 2
        + [dma((3,))],
        compiler_params=pltpu.CompilerParams(
            vmem_limit_bytes=VMEM_LIMIT, collective_id=1, has_side_effects=True
        ),
        name="mixer",
    )(projected, both, raw, decay_rate[None], skip_gain[None], out_weight)


def solution(mesh):
    in_specs = (
        P("seq", "tp"),
        P(None, None, "tp"),
        P(None, "tp"),
        P(None, None, "tp"),
        P(None, "tp"),
        P("tp"),
        P("tp"),
        P("tp", None),
    )
    out_specs = P("seq", "tp")
    return jax.shard_map(shards, mesh=mesh, in_specs=in_specs, out_specs=out_specs, check_vma=False)
```

time: 65.2 us -> 49.2 us (0.75)
  Pallas kernels: 47.8 us -> 36.5 us
  matrix products: 10.5 us -> 7.66 us
  local copies, waits for them, and re-layouts: 5.71 us -> 4.83 us
  other arithmetic: 0.8 us -> 0 us
    pallas_call x3 -> x1, Pallas kernels: 43 us -> 31.4 us  [shards(): pl.pallas_call(functools.partial(mixer_kernel, outer, n), out_shape=jax.S...]
    dot_general x1, matrix products: 10.5 us -> 7.66 us  [shards(): jnp.einsum('td,dkf->ktf', whole, in_weight, preferred_element_type=F32)]
    broadcast_in_dim x1 -> x0, other arithmetic: 0.8 us -> none  [shards(): rate = jnp.concatenate([decay_rate, decay_rate])[None, :]]
    reshape x1 -> x0, local copies, waits for them, and re-layouts: 0.76 us -> none  [shards(): dt_bias.reshape(1, 2 * heads)]
    broadcast_in_dim x1 -> x0, local copies, waits for them, and re-layouts: 0.72 us -> none  [shards(): gain = jnp.repeat(skip_gain, HEAD_DIM)[None, :]]
    unnamed x7 -> x13, local copies, waits for them, and re-layouts: 4.14 us -> 4.83 us
where the time goes in v3:
time: 49.2 us; the launch traced here: 49 us
  Pallas kernels  36.5 us (74%)
  matrix products  7.66 us (16%)
  local copies, waits for them, and re-layouts  4.83 us (10%)
    pallas_call x1, Pallas kernels, shards(): pl.pallas_call(functools.partial(mixer_kernel, outer, n), out_shape=jax.S...  31.4 us
    dot_general x1, matrix products, shards(): jnp.einsum('td,dkf->ktf', whole, in_weight, preferred_element_type=F32)  7.66 us
    pallas_call x1, Pallas kernels, shards(): pl.pallas_call(functools.partial(gather_kernel, n), out_shape=(jax.ShapeD...  5.06 us
    unnamed x13, local copies, waits for them, and re-layouts  4.83 us

profile of v3, /device:TPU:0, one launch (start us, length us, event | category | flops | bytes accessed | tf_op | source)
XLA Modules:
  0.0 49.0 jit_solution(16606461789625043889)
XLA Ops:
  0.0 0.0 copy-start
  0.0 1.2 %copy-done = bf16[512,1024]{1,0:T(8,128)(2,1)S(1)} copy-done((bf16[512,1024]{1,0:T(8,128)(2,1)S(1)}, bf16[512,1024]{1,0:T(8,128)(2,1)}, u32[]{:S(2)}) %copy-start) | copy-done | bytes 1048600
  1.2 0.0 copy-start.1
  1.2 1.0 %copy-done.1 = bf16[2048,128]{1,0:T(8,128)(2,1)S(1)} copy-done((bf16[2048,128]{1,0:T(8,128)(2,1)S(1)}, bf16[2048,128]{1,0:T(8,128)(2,1)}, u32[]{:S(2)}) %copy-start.1) | copy-done | bytes 524312
  2.3 0.0 copy-start.2
  2.3 0.9 %copy-done.2 = bf16[2,2048,16]{1,2,0:T(8,128)(2,1)S(1)} copy-done((bf16[2,2048,16]{1,2,0:T(8,128)(2,1)S(1)}, bf16[2,2048,16]{1,2,0:T(8,128)(2,1)}, u32[]{:S(2)}) %copy-start.2) | copy-done | bytes 131096
  3.2 0.0 copy-start.3
  3.2 0.7 %copy-done.3 = f32[2,16]{1,0:T(2,128)S(1)} copy-done((f32[2,16]{1,0:T(2,128)S(1)}, f32[2,16]{1,0:T(2,128)}, u32[]{:S(2)}) %copy-start.3) | copy-done | bytes 152
  3.9 5.1 %gather_features.1 = (bf16[512,2048]{1,0:T(8,128)(2,1)S(1)}, bf16[512,256]{1,0:T(8,128)(2,1)S(1)}, f32[512,32]{1,0:T(8,128)S(1)}) custom-call(bf16[512,1024]{1,0:T(8,128)(2,1)S(1)} %copy-done, bf16[2048,128]{1,0:T(8,128)(2,1)S(1)} %copy-done.1, bf16[32,2048]{1,0:T(8,128)(2,1)S(1)} %bitcast.10, f32[2,16]{1,0:T(2,128)S(1)} %copy-done.3), custom_call_target="tpu_custom_call" | custom-call | tf_op jit(solution)/shard_map/gather_features/pallas_call | solution.py:404
  8.9 0.0 copy-start.4
  8.9 0.0 copy-start.5
  8.9 7.7 %fusion.2.proj_ref = f32[2,512,1024]{2,1,0:T(8,128)S(1)} fusion(bf16[2048,2,1024]{2,1,0:T(2,128)(2,1)} %param.9, bf16[512,2048]{1,0:T(8,128)(2,1)S(1)} %get-tuple-element.8), kind=kOutput, calls=%fused_computation.2 | convolution fusion | flops 4294967296 | bytes 14680064 | tf_op jit(solution)/shard_map/td,dkf->ktf/dot_general | solution.py:429
  16.6 0.0 copy-done.4
  16.6 0.0 copy-done.5
  16.6 31.4 %mixer.1 = bf16[512,1024]{1,0:T(8,128)(2,1)S(1)} custom-call(f32[2,512,1024]{2,1,0:T(8,128)S(1)} %fusion.2.proj_ref, bf16[512,256]{1,0:T(8,128)(2,1)S(1)} %get-tuple-element.9.both_ref, f32[512,32]{1,0:T(8,128)S(1)} %get-tuple-element.10.raw_ref, f32[1,16]{1,0:T(1,128)S(1)} %bitcast.11, f32[1,16]{1,0:T(1,128)S(1)} %bitcast.12, bf16[1024,2048]{1,0:T(8,128)(2,1)} %weight_hbm.1), custom_call_target="tpu_custom_call" | custom-call | tf_op jit(solution)/shard_map/mixer/pallas_call | solution.py:430
  48.0 1.0 %copy.15 = bf16[512,1024]{1,0:T(8,128)(2,1)} copy(bf16[512,1024]{1,0:T(8,128)(2,1)S(1)} %mixer.1) | data formatting | bytes 2097152
Async XLA Ops:
  0.0 1.2 %copy-start = (bf16[512,1024]{1,0:T(8,128)(2,1)S(1)}, bf16[512,1024]{1,0:T(8,128)(2,1)}, u32[]{:S(2)}) copy-start(bf16[512,1024]{1,0:T(8,128)(2,1)} %tokens_ref.1) | copy-start | bytes 3145732
  1.2 1.0 %copy-start.1 = (bf16[2048,128]{1,0:T(8,128)(2,1)S(1)}, bf16[2048,128]{1,0:T(8,128)(2,1)}, u32[]{:S(2)}) copy-start(bf16[2048,128]{1,0:T(8,128)(2,1)} %bc_ref.1) | copy-start | bytes 1572868
  2.3 0.9 %copy-start.2 = (bf16[2,2048,16]{1,2,0:T(8,128)(2,1)S(1)}, bf16[2,2048,16]{1,2,0:T(8,128)(2,1)}, u32[]{:S(2)}) copy-start(bf16[2,2048,16]{1,2,0:T(8,128)(2,1)} %param.11) | copy-start | bytes 393220
  3.2 0.7 %copy-start.3 = (f32[2,16]{1,0:T(2,128)S(1)}, f32[2,16]{1,0:T(2,128)}, u32[]{:S(2)}) copy-start(f32[2,16]{1,0:T(2,128)} %bias_ref.1) | copy-start | bytes 388
  8.9 7.7 %copy-start.4 = (f32[16]{0:T(128)S(1)}, f32[16]{0:T(128)}, u32[]{:S(2)}) copy-start(f32[16]{0:T(128)} %param.13) | copy-start | bytes 196
  8.9 7.7 %copy-start.5 = (f32[16]{0:T(128)S(1)}, f32[16]{0:T(128)}, u32[]{:S(2)}) copy-start(f32[16]{0:T(128)} %param.14) | copy-start | bytes 196

commit v4 on v3

--- a/solution.py
+++ b/solution.py
@@ -12,7 +12,8 @@
 CHUNK = 128
 GROUP = 4
 PARTS = 4
-VMEM_LIMIT = 48 * 1024 * 1024
+VMEM_LIMIT = 40 * 1024 * 1024
+GATHER_LIMIT = 60 * 1024 * 1024
 F32 = jnp.float32
 BF16 = jnp.bfloat16
 HIGH = lax.Precision.HIGHEST
@@ -108,11 +109,13 @@
     rate_ref,
     gain_ref,
     weight_hbm,
-    out_ref,
+    own,
+    arrived,
     values_wide,
     gates,
     weight_ref,
-    sums,
+    weighted,
+    turned,
     local,
     mix,
     send_ref,
@@ -127,9 +130,7 @@
     back,
     landed,
     hidden,
-    own,
     leaving,
-    arrived,
     send1,
     recv1,
     send2,
@@ -148,7 +149,7 @@
     width = heads * HEAD_DIM
     chunks = raw_ref.shape[0] // CHUNK
     quarter = width // GROUP
-    columns = out_ref.shape[1]
+    columns = own.shape[1]
 
     get_values = pltpu.make_async_copy(proj_ref.at[0], values_wide, here_sem.at[0])
     get_gates = pltpu.make_async_copy(proj_ref.at[1], gates, here_sem.at[1])
@@ -222,34 +223,93 @@
     for c in range(chunks):
         rows = slice(c * CHUNK, (c + 1) * CHUNK)
         values = values_wide[rows, :].astype(BF16).astype(F32)
-        weighted = jnp.concatenate([values, values], axis=1) * spread_chunk(weight, c)
-        sums[c] = dot(both_ref[rows, :STATE], weighted.astype(BF16), ((0,), (0,)))
+        wide = jnp.concatenate([values, values], axis=1) * spread_chunk(weight, c)
+        weighted[c] = wide.astype(BF16)
+        turned[c] = both_ref[rows, :STATE].T
+
+    def block_state(rows):
+        for way in range(2):
+            side = slice(way * width, (way + 1) * width)
+            carry = jnp.zeros((rows.stop - rows.start, width), F32)
+            for c in range(chunks) if way == 0 else range(chunks - 1, -1, -1):
+                local[c, rows, side] = carry.astype(BF16)
+                new = dot(turned[c, rows, :], weighted[c, :, side])
+                carry = jnp.exp(totals[c : c + 1, side]) * carry + new
+            for q in range(GROUP):
+                part = slice(q * quarter, (q + 1) * quarter)
+                send_ref[q, way, rows, :] = carry[:, part].astype(BF16)
+
     for way in range(2):
-        side = slice(way * width, (way + 1) * width)
-        carry = jnp.zeros((STATE, width), F32)
-        for c in range(chunks) if way == 0 else range(chunks - 1, -1, -1):
-            local[c, :, side] = carry.astype(BF16)
-            carry = jnp.exp(totals[c : c + 1, side]) * carry + sums[c, :, side]
         for q in range(GROUP):
-            part = slice(q * quarter, (q + 1) * quarter)
-            send_ref[q, way] = carry[:, part].astype(BF16)
-            total = totals[chunks : chunks + 1, side][:, part]
-            total_ref[q, way] = jnp.broadcast_to(total, (8, quarter))
-
-    pl.semaphore_wait(barrier, GROUP - 1 + outer - 1 + n - 1)
+            part = slice(way * width + q * quarter, way * width + (q + 1) * quarter)
+            total_ref[q, way] = jnp.broadcast_to(totals[chunks : chunks + 1, part], (8, quarter))
 
     bands = [pl.ds(p * (STATE // PARTS), STATE // PARTS) for p in range(PARTS)]
-
     first = [[] for _ in bands]
-    for d in range(1, GROUP):
-        to = (g + d) % GROUP
-        first[0].append(push(total_ref.at[to], got_total.at[g], send1, recv1, d - 1, peer(z, to)))
-    for p, band in enumerate(bands):
+    second = [[] for _ in bands]
+    third = []
+    before_state = [[None] * GROUP, [None] * GROUP]
+
+    def share(p):
         for d in range(1, GROUP):
             to = (g + d) % GROUP
+            if p == 0:
+                total = total_ref.at[to]
+                first[p].append(push(total, got_total.at[g], send1, recv1, d - 1, peer(z, to)))
             slot = (p + 1) * (GROUP - 1) + d - 1
-            source = send_ref.at[to, :, band, :]
-            first[p].append(push(source, got.at[g, :, band, :], send1, recv1, slot, peer(z, to)))
+            source = send_ref.at[to, :, bands[p], :]
+            target = got.at[g, :, bands[p], :]
+            first[p].append(push(source, target, send1, recv1, slot, peer(z, to)))
+
+    def along(p):
+        band = bands[p]
+        for copy in first[p]:
+            copy.wait()
+        for way in range(2):
+            carry = jnp.zeros((STATE // PARTS, quarter), F32)
+            gone = jnp.zeros((8, quarter), F32)
+            for s in range(GROUP) if way == 0 else range(GROUP - 1, -1, -1):
+                inner[s, way, band, :] = carry
+                before_state[way][s] = jnp.exp(gone[:1])
+                carry = jnp.exp(got_total[s, way][:1]) * carry + got[s, way, band, :].astype(F32)
+                gone = gone + got_total[s, way]
+            group[way, band, :] = carry.astype(BF16)
+            if p == 0:
+                group_total[way] = gone
+        for d in range(1, outer):
+            way = (z + d) // outer
+            to = peer((z + d) % outer, g)
+            if p == 0:
+                total = group_total.at[way]
+                second[p].append(push(total, far_total.at[z], send2, recv2, d - 1, to))
+            slot = (p + 1) * (outer - 1) + d - 1
+            source = group.at[way, band, :]
+            second[p].append(push(source, far.at[z, band, :], send2, recv2, slot, to))
+
+    def hand_back(p):
+        band = bands[p]
+        for copy in second[p]:
+            copy.wait()
+        for way in range(2):
+            carry = jnp.zeros((STATE // PARTS, quarter), F32)
+            for s in range(outer) if way == 0 else range(outer - 1, -1, -1):
+                longer = jnp.exp(far_total[s][:1]) * carry + far[s, band, :].astype(F32)
+                carry = jnp.where(s < z if way == 0 else s > z, longer, carry)
+            for s in range(GROUP):
+                entering = inner[s, way, band, :] + before_state[way][s] * carry
+                back[s, way, band, :] = entering.astype(BF16)
+        for d in range(1, GROUP):
+            to = (g + d) % GROUP
+            slot = p * (GROUP - 1) + d - 1
+            source = back.at[to, :, band, :]
+            third.append(push(source, landed.at[g, :, band, :], send3, recv3, slot, peer(z, to)))
+
+    half = STATE // 2
+    block_state(slice(0, half))
+    pl.semaphore_wait(barrier, GROUP - 1 + outer - 1 + n - 1)
+    share(0)
+    share(1)
+    block_state(slice(half, STATE))
     got[g] = send_ref[g]
     got_total[g] = total_ref[g]
     far[z] = jnp.zeros(far.shape[1:], BF16)
@@ -292,62 +352,32 @@
         values = values_wide[rows, :].astype(BF16).astype(F32)
         mix[rows, :] = mix[rows, :] + reach[:, :width] + reach[:, width:] + gain * values
 
+    def activate(c):
+        rows = slice(c * CHUNK, (c + 1) * CHUNK)
+        gates[rows, :] = gates[rows, :] / (1.0 + jnp.exp(-gates[rows, :]))
+
     inside(0)
-    if chunks > 1:
-        inside(1)
-    before_state = [[None] * GROUP, [None] * GROUP]
-    second = [[] for _ in bands]
-    for p, band in enumerate(bands):
-        for copy in first[p]:
-            copy.wait()
-        for way in range(2):
-            carry = jnp.zeros((STATE // PARTS, quarter), F32)
-            gone = jnp.zeros((8, quarter), F32)
-            for s in range(GROUP) if way == 0 else range(GROUP - 1, -1, -1):
-                inner[s, way, band, :] = carry
-                before_state[way][s] = jnp.exp(gone[:1])
-                carry = jnp.exp(got_total[s, way][:1]) * carry + got[s, way, band, :].astype(F32)
-                gone = gone + got_total[s, way]
-            group[way, band, :] = carry.astype(BF16)
-            if p == 0:
-                group_total[way] = gone
-
-        for d in range(1, outer):
-            way = (z + d) // outer
-            to = peer((z + d) % outer, g)
-            if p == 0:
-                total = group_total.at[way]
-                second[p].append(push(total, far_total.at[z], send2, recv2, d - 1, to))
-            slot = (p + 1) * (outer - 1) + d - 1
-            source = group.at[way, band, :]
-            second[p].append(push(source, far.at[z, band, :], send2, recv2, slot, to))
-
-    for c in range(2, chunks):
-        inside(c)
-    third = []
-    for p, band in enumerate(bands):
-        for copy in second[p]:
-            copy.wait()
-        for way in range(2):
-            carry = jnp.zeros((STATE // PARTS, quarter), F32)
-            for s in range(outer) if way == 0 else range(outer - 1, -1, -1):
-                longer = jnp.exp(far_total[s][:1]) * carry + far[s, band, :].astype(F32)
-                carry = jnp.where(s < z if way == 0 else s > z, longer, carry)
-            for s in range(GROUP):
-                entering = inner[s, way, band, :] + before_state[way][s] * carry
-                back[s, way, band, :] = entering.astype(BF16)
-
-        for d in range(1, GROUP):
-            to = (g + d) % GROUP
-            slot = p * (GROUP - 1) + d - 1
-            source = back.at[to, :, band, :]
-            third.append(push(source, landed.at[g, :, band, :], send3, recv3, slot, peer(z, to)))
+    along(0)
+    share(2)
+    inside(1)
+    along(1)
+    share(3)
+    inside(2)
+    along(2)
+    hand_back(0)
+    inside(3)
+    along(3)
+    hand_back(1)
+    nearby(0)
+    nearby(1)
+    hand_back(2)
+    nearby(2)
+    nearby(3)
+    hand_back(3)
     landed[g] = back[g]
     get_gates.wait()
     for c in range(chunks):
-        nearby(c)
-        rows = slice(c * CHUNK, (c + 1) * CHUNK)
-        gates[rows, :] = gates[rows, :] / (1.0 + jnp.exp(-gates[rows, :]))
+        activate(c)
     get_weight.wait()
     for copy in third:
         copy.wait()
@@ -378,14 +408,10 @@
             copies.append(
                 push(source, arrived.at[d - 1, rows, :], send4, recv4, slot, {"tp": to})
             )
-        mine = pl.ds(pl.multiple_of(me * columns, columns), columns)
-        own[rows, :] = dot(hidden[rows, :], weight_ref[:, mine]).astype(BF16)
+    mine = pl.ds(pl.multiple_of(me * columns, columns), columns)
+    own[...] = dot(hidden[...], weight_ref[:, mine]).astype(BF16)
     for copy in copies:
         copy.wait()
-    total = own[...].astype(F32)
-    for d in range(1, n):
-        total = total + arrived[d - 1].astype(F32)
-    out_ref[...] = total.astype(BF16)
 
 
 def shards(tokens, in_weight, bc_weight, dt_weight, dt_bias, decay_rate, skip_gain, out_weight):
@@ -417,7 +443,7 @@
         + [dma((n - 1,))] * 4
         + [dma((3,))],
         compiler_params=pltpu.CompilerParams(
-            vmem_limit_bytes=VMEM_LIMIT, collective_id=0, has_side_effects=True
+            vmem_limit_bytes=GATHER_LIMIT, collective_id=0, has_side_effects=True
         ),
         name="gather_features",
     )(
@@ -427,16 +453,20 @@
         dt_bias,
     )
     projected = jnp.einsum("td,dkf->ktf", whole, in_weight, preferred_element_type=F32)
-    return pl.pallas_call(
+    own, arrived = pl.pallas_call(
         functools.partial(mixer_kernel, outer, n),
-        out_shape=jax.ShapeDtypeStruct((length, columns), BF16),
+        out_shape=(
+            jax.ShapeDtypeStruct((length, columns), BF16),
+            jax.ShapeDtypeStruct((n - 1, length, columns), BF16),
+        ),
         in_specs=[anywhere, vmem, vmem, vmem, vmem, anywhere],
-        out_specs=vmem,
+        out_specs=(vmem, vmem),
         scratch_shapes=[
             pltpu.VMEM((length, width), F32),
             pltpu.VMEM((length, width), F32),
             pltpu.VMEM(out_weight.shape, BF16),
-            pltpu.VMEM((chunks, STATE, 2 * width), F32),
+            pltpu.VMEM((chunks, CHUNK, 2 * width), BF16),
+            pltpu.VMEM((chunks, STATE, CHUNK), BF16),
             pltpu.VMEM((chunks, STATE, 2 * width), BF16),
             pltpu.VMEM((length, width), F32),
             pltpu.VMEM((GROUP, 2, STATE, quarter), BF16),
@@ -451,8 +481,6 @@
             pltpu.VMEM((GROUP, 2, STATE, quarter), BF16),
             pltpu.VMEM((GROUP, 2, STATE, quarter), BF16),
             pltpu.VMEM((length, width), BF16),
-            pltpu.VMEM((length, columns), BF16),
-            pltpu.VMEM((n - 1, length, columns), BF16),
             pltpu.VMEM((n - 1, length, columns), BF16),
         ]
         + [dma(((PARTS + 1) * (GROUP - 1),))] * 2
@@ -465,6 +493,10 @@
         ),
         name="mixer",
     )(projected, both, raw, decay_rate[None], skip_gain[None], out_weight)
+    total = own.astype(F32)
+    for d in range(n - 1):
+        total = total + arrived[d].astype(F32)
+    return total.astype(BF16)
 
 
 def solution(mesh):

time: 49.2 us -> 48.2 us (0.980)
  local copies, waits for them, and re-layouts: 4.83 us -> 0.03 us
  Pallas kernels: 36.5 us -> 38 us
  other arithmetic: 0 us -> 1.37 us
  matrix products: 7.66 us -> 8.48 us
    unnamed x13 -> x10, local copies, waits for them, and re-layouts: 4.83 us -> 0.03 us
    convert_element_type x0 -> x1, other arithmetic: none -> 1.37 us  [shards(): return total.astype(BF16)]
    pallas_call x1, Pallas kernels: 5.06 us -> 6.42 us  [shards(): pl.pallas_call(functools.partial(gather_kernel, n), out_shape=(jax.ShapeD...]
    dot_general x1, matrix products: 7.66 us -> 8.48 us  [shards(): jnp.einsum('td,dkf->ktf', whole, in_weight, preferred_element_type=F32)]
where the time goes in v4:
time: 48.2 us; the launch traced here: 48 us
  Pallas kernels  38 us (79%)
  matrix products  8.48 us (18%)
  other arithmetic  1.37 us (3%)
    pallas_call x1, Pallas kernels, shards(): pl.pallas_call(functools.partial(mixer_kernel, outer, n), out_shape=(jax....  31.6 us
    dot_general x1, matrix products, shards(): jnp.einsum('td,dkf->ktf', whole, in_weight, preferred_element_type=F32)  8.48 us
    pallas_call x1, Pallas kernels, shards(): pl.pallas_call(functools.partial(gather_kernel, n), out_shape=(jax.ShapeD...  6.42 us
    convert_element_type x1, other arithmetic, shards(): return total.astype(BF16)  1.37 us

profile of v4, /device:TPU:0, one launch (start us, length us, event | category | flops | bytes accessed | tf_op | source)
XLA Modules:
  0.0 48.0 jit_solution(11878659849375131131)
XLA Ops:
  0.0 6.4 %gather_features.1 = (bf16[512,2048]{1,0:T(8,128)(2,1)}, bf16[512,256]{1,0:T(8,128)(2,1)}, f32[512,32]{1,0:T(8,128)}) custom-call(bf16[512,1024]{1,0:T(8,128)(2,1)} %tokens_ref.1, bf16[2048,128]{1,0:T(8,128)(2,1)} %bc_ref.1, bf16[32,2048]{1,0:T(8,128)(2,1)} %bitcast.15, f32[2,16]{1,0:T(2,128)} %bias_ref.1), custom_call_target="tpu_custom_call" | custom-call | tf_op jit(solution)/shard_map/gather_features/pallas_call | solution.py:430
  6.4 0.0 copy-start
  6.4 0.0 copy-start.1
  6.4 0.0 copy-start.2
  6.5 0.0 copy-start.3
  6.5 0.0 copy-start.4
  6.5 8.5 %fusion.2.proj_ref = f32[2,512,1024]{2,1,0:T(8,128)S(1)} fusion(bf16[2048,2,1024]{2,1,0:T(2,128)(2,1)} %param.9, bf16[512,2048]{1,0:T(8,128)(2,1)} %get-tuple-element.10), kind=kOutput, calls=%fused_computation.2 | convolution fusion | flops 4294967296 | bytes 14680064 | tf_op jit(solution)/shard_map/td,dkf->ktf/dot_general | solution.py:455
  15.0 0.0 copy-done
  15.0 0.0 copy-done.1
  15.0 0.0 copy-done.2
  15.0 0.0 copy-done.3
  15.0 0.0 copy-done.4
  15.0 31.6 %mixer.1 = (bf16[512,1024]{1,0:T(8,128)(2,1)S(1)}, bf16[1,512,1024]{2,1,0:T(8,128)(2,1)S(1)}) custom-call(f32[2,512,1024]{2,1,0:T(8,128)S(1)} %fusion.2.proj_ref, bf16[512,256]{1,0:T(8,128)(2,1)S(1)} %copy-done.1, f32[512,32]{1,0:T(8,128)S(1)} %copy-done.2, f32[1,16]{1,0:T(1,128)S(1)} %bitcast.13, f32[1,16]{1,0:T(1,128)S(1)} %bitcast.14, ...), custom_call_target="tpu_custom_call" | custom-call | tf_op jit(solution)/shard_map/mixer/pallas_call | solution.py:456
  46.6 1.4 %fusion.5 = bf16[512,1024]{1,0:T(8,128)(2,1)} fusion(bf16[512,1024]{1,0:T(8,128)(2,1)S(1)} %get-tuple-element.13, bf16[1,512,1024]{2,1,0:T(8,128)(2,1)S(1)} %get-tuple-element.14), kind=kLoop, calls=%fused_computation.4 | loop fusion | flops 2097152 | bytes 3145728 | tf_op jit(solution)/shard_map/convert_element_type | solution.py:499
Async XLA Ops:
  6.4 8.5 %copy-start = (bf16[1024,2048]{1,0:T(8,128)(2,1)S(1)}, bf16[1024,2048]{1,0:T(8,128)(2,1)}, u32[]{:S(2)}) copy-start(bf16[1024,2048]{1,0:T(8,128)(2,1)} %weight_hbm.1) | copy-start | bytes 12582916
  6.4 8.5 %copy-start.1 = (bf16[512,256]{1,0:T(8,128)(2,1)S(1)}, bf16[512,256]{1,0:T(8,128)(2,1)}, u32[]{:S(2)}) copy-start(bf16[512,256]{1,0:T(8,128)(2,1)} %get-tuple-element.11.both_ref) | copy-start | bytes 786436
  6.4 8.5 %copy-start.2 = (f32[512,32]{1,0:T(8,128)S(1)}, f32[512,32]{1,0:T(8,128)}, u32[]{:S(2)}) copy-start(f32[512,32]{1,0:T(8,128)} %get-tuple-element.12.raw_ref) | copy-start | bytes 196612
  6.5 8.5 %copy-start.3 = (f32[16]{0:T(128)S(1)}, f32[16]{0:T(128)}, u32[]{:S(2)}) copy-start(f32[16]{0:T(128)} %param.13) | copy-start | bytes 196
  6.5 8.5 %copy-start.4 = (f32[16]{0:T(128)S(1)}, f32[16]{0:T(128)}, u32[]{:S(2)}) copy-start(f32[16]{0:T(128)} %param.14) | copy-start | bytes 196

commit v5 on v4

--- a/solution.py
+++ b/solution.py
@@ -14,6 +14,7 @@
 PARTS = 4
 VMEM_LIMIT = 40 * 1024 * 1024
 GATHER_LIMIT = 60 * 1024 * 1024
+LOG2_E = 1.4426950408889634
 F32 = jnp.float32
 BF16 = jnp.bfloat16
 HIGH = lax.Precision.HIGHEST
@@ -130,6 +131,7 @@
     back,
     landed,
     hidden,
+    scales,
     leaving,
     send1,
     recv1,
@@ -151,10 +153,14 @@
     quarter = width // GROUP
     columns = own.shape[1]
 
-    get_values = pltpu.make_async_copy(proj_ref.at[0], values_wide, here_sem.at[0])
-    get_gates = pltpu.make_async_copy(proj_ref.at[1], gates, here_sem.at[1])
-    get_weight = pltpu.make_async_copy(weight_hbm, weight_ref, here_sem.at[2])
-    get_values.start()
+    get_values = []
+    for c in range(chunks):
+        rows = pl.ds(c * CHUNK, CHUNK)
+        source = proj_ref.at[0, rows, :]
+        get_values.append(pltpu.make_async_copy(source, values_wide.at[rows, :], here_sem.at[c]))
+        get_values[c].start()
+    get_gates = pltpu.make_async_copy(proj_ref.at[1], gates, here_sem.at[chunks])
+    get_weight = pltpu.make_async_copy(weight_hbm, weight_ref, here_sem.at[chunks + 1])
     get_gates.start()
     get_weight.start()
 
@@ -194,8 +200,8 @@
     last = upto[CHUNK - 1 : CHUNK, :]
     forward = lax.rem(lax.broadcasted_iota(jnp.int32, (CHUNK, every), 1), heads2) < heads
     weight = jnp.exp(jnp.where(forward, last - upto, before)) * steps
-    column = jnp.where(forward, before, -upto)
-    row = (jnp.where(forward, -upto, before) + jnp.log(steps)).T
+    column = LOG2_E * jnp.where(forward, before, -upto)
+    row = (LOG2_E * (jnp.where(forward, -upto, before) + jnp.log(steps))).T
     scale = jnp.exp(jnp.where(forward, before, last - upto))
     lasts = [last[:, c * heads2 : (c + 1) * heads2] for c in range(chunks)]
     passed = []
@@ -219,8 +225,8 @@
     def spread_chunk(value, c):
         return dot(split_wide(value[:, c * heads2 : (c + 1) * heads2]), spread)
 
-    get_values.wait()
     for c in range(chunks):
+        get_values[c].wait()
         rows = slice(c * CHUNK, (c + 1) * CHUNK)
         values = values_wide[rows, :].astype(BF16).astype(F32)
         wide = jnp.concatenate([values, values], axis=1) * spread_chunk(weight, c)
@@ -310,6 +316,8 @@
     share(0)
     share(1)
     block_state(slice(half, STATE))
+    share(2)
+    share(3)
     got[g] = send_ref[g]
     got_total[g] = total_ref[g]
     far[z] = jnp.zeros(far.shape[1:], BF16)
@@ -333,7 +341,7 @@
                     column[:, b : b + 1] + row[b : b + 1, :],
                 )
                 power = jnp.where(on_line, -jnp.inf, power)
-                weights.append((scores * jnp.exp(power)).astype(BF16))
+                weights.append((scores * jnp.exp2(power)).astype(BF16))
             lanes = slice(pair * 2 * HEAD_DIM, (pair + 1) * 2 * HEAD_DIM)
             pair_values = values_wide[rows, lanes].astype(BF16)
             zero = jnp.zeros_like(pair_values)
@@ -356,28 +364,27 @@
         rows = slice(c * CHUNK, (c + 1) * CHUNK)
         gates[rows, :] = gates[rows, :] / (1.0 + jnp.exp(-gates[rows, :]))
 
+    def spread_scale(c):
+        scales[c] = spread_chunk(enter_scale, c)
+
     inside(0)
     along(0)
-    share(2)
+    along(1)
     inside(1)
-    along(1)
-    share(3)
+    along(2)
+    along(3)
+    hand_back(0)
     inside(2)
-    along(2)
-    hand_back(0)
+    hand_back(1)
+    hand_back(2)
     inside(3)
-    along(3)
-    hand_back(1)
-    nearby(0)
-    nearby(1)
-    hand_back(2)
-    nearby(2)
-    nearby(3)
     hand_back(3)
     landed[g] = back[g]
     get_gates.wait()
     for c in range(chunks):
+        nearby(c)
         activate(c)
+        spread_scale(c)
     get_weight.wait()
     for copy in third:
         copy.wait()
@@ -387,7 +394,7 @@
         rows = slice(c * CHUNK, (c + 1) * CHUNK)
         queries = both_ref[rows, STATE:]
         reach = [dot(queries, landed[q, way]) for way in range(2) for q in range(GROUP)]
-        reach = jnp.concatenate(reach, axis=1) * spread_chunk(enter_scale, c)
+        reach = jnp.concatenate(reach, axis=1) * scales[c]
         gated = (mix[rows, :] + reach[:, :width] + reach[:, width:]) * gates[rows, :]
         square = gated * gated
         high = square.astype(BF16)
@@ -481,13 +488,14 @@
             pltpu.VMEM((GROUP, 2, STATE, quarter), BF16),
             pltpu.VMEM((GROUP, 2, STATE, quarter), BF16),
             pltpu.VMEM((length, width), BF16),
+            pltpu.VMEM((chunks, CHUNK, 2 * width), F32),
             pltpu.VMEM((n - 1, length, columns), BF16),
         ]
         + [dma(((PARTS + 1) * (GROUP - 1),))] * 2
         + [dma(((PARTS + 1) * (outer - 1),))] * 2
         + [dma((PARTS * (GROUP - 1),))] * 2
         + [dma((chunks // 2 * (n - 1),))] * 2
-        + [dma((3,))],
+        + [dma((chunks + 2,))],
         compiler_params=pltpu.CompilerParams(
             vmem_limit_bytes=VMEM_LIMIT, collective_id=1, has_side_effects=True
         ),

time: 48.2 us -> 46.5 us (0.965)
  Pallas kernels: 38 us -> 36.3 us
    pallas_call x1, Pallas kernels: 31.6 us -> 29.9 us  [shards(): pl.pallas_call(functools.partial(mixer_kernel, outer, n), out_shape=(jax....]
where the time goes in v5:
time: 46.5 us; the launch traced here: 46.3 us
  Pallas kernels  36.3 us (78%)
  matrix products  8.48 us (18%)
  other arithmetic  1.37 us (3%)
    pallas_call x1, Pallas kernels, shards(): pl.pallas_call(functools.partial(mixer_kernel, outer, n), out_shape=(jax....  29.9 us
    dot_general x1, matrix products, shards(): jnp.einsum('td,dkf->ktf', whole, in_weight, preferred_element_type=F32)  8.48 us
    pallas_call x1, Pallas kernels, shards(): pl.pallas_call(functools.partial(gather_kernel, n), out_shape=(jax.ShapeD...  6.42 us
    convert_element_type x1, other arithmetic, shards(): return total.astype(BF16)  1.37 us

profile of v5, /device:TPU:0, one launch (start us, length us, event | category | flops | bytes accessed | tf_op | source)
XLA Modules:
  0.0 46.3 jit_solution(4336100764195148856)
XLA Ops:
  0.0 6.4 %gather_features.1 = (bf16[512,2048]{1,0:T(8,128)(2,1)}, bf16[512,256]{1,0:T(8,128)(2,1)}, f32[512,32]{1,0:T(8,128)}) custom-call(bf16[512,1024]{1,0:T(8,128)(2,1)} %tokens_ref.1, bf16[2048,128]{1,0:T(8,128)(2,1)} %bc_ref.1, bf16[32,2048]{1,0:T(8,128)(2,1)} %bitcast.15, f32[2,16]{1,0:T(2,128)} %bias_ref.1), custom_call_target="tpu_custom_call" | custom-call | tf_op jit(solution)/shard_map/gather_features/pallas_call | solution.py:437
  6.4 0.0 copy-start
  6.4 0.0 copy-start.1
  6.4 0.0 copy-start.2
  6.5 0.0 copy-start.3
  6.5 0.0 copy-start.4
  6.5 8.5 %fusion.2.proj_ref = f32[2,512,1024]{2,1,0:T(8,128)S(1)} fusion(bf16[2048,2,1024]{2,1,0:T(2,128)(2,1)} %param.9, bf16[512,2048]{1,0:T(8,128)(2,1)} %get-tuple-element.10), kind=kOutput, calls=%fused_computation.2 | convolution fusion | flops 4294967296 | bytes 14680064 | tf_op jit(solution)/shard_map/td,dkf->ktf/dot_general | solution.py:462
  15.0 0.0 copy-done
  15.0 0.0 copy-done.1
  15.0 0.0 copy-done.2
  15.0 0.0 copy-done.3
  15.0 0.0 copy-done.4
  15.0 29.9 %mixer.1 = (bf16[512,1024]{1,0:T(8,128)(2,1)S(1)}, bf16[1,512,1024]{2,1,0:T(8,128)(2,1)S(1)}) custom-call(f32[2,512,1024]{2,1,0:T(8,128)S(1)} %fusion.2.proj_ref, bf16[512,256]{1,0:T(8,128)(2,1)S(1)} %copy-done.1, f32[512,32]{1,0:T(8,128)S(1)} %copy-done.2, f32[1,16]{1,0:T(1,128)S(1)} %bitcast.13, f32[1,16]{1,0:T(1,128)S(1)} %bitcast.14, ...), custom_call_target="tpu_custom_call" | custom-call | tf_op jit(solution)/shard_map/mixer/pallas_call | solution.py:463
  44.9 1.4 %fusion.5 = bf16[512,1024]{1,0:T(8,128)(2,1)} fusion(bf16[512,1024]{1,0:T(8,128)(2,1)S(1)} %get-tuple-element.13, bf16[1,512,1024]{2,1,0:T(8,128)(2,1)S(1)} %get-tuple-element.14), kind=kLoop, calls=%fused_computation.4 | loop fusion | flops 2097152 | bytes 3145728 | tf_op jit(solution)/shard_map/convert_element_type | solution.py:507
Async XLA Ops:
  6.4 8.5 %copy-start = (bf16[1024,2048]{1,0:T(8,128)(2,1)S(1)}, bf16[1024,2048]{1,0:T(8,128)(2,1)}, u32[]{:S(2)}) copy-start(bf16[1024,2048]{1,0:T(8,128)(2,1)} %weight_hbm.1) | copy-start | bytes 12582916
  6.4 8.5 %copy-start.1 = (bf16[512,256]{1,0:T(8,128)(2,1)S(1)}, bf16[512,256]{1,0:T(8,128)(2,1)}, u32[]{:S(2)}) copy-start(bf16[512,256]{1,0:T(8,128)(2,1)} %get-tuple-element.11.both_ref) | copy-start | bytes 786436
  6.4 8.5 %copy-start.2 = (f32[512,32]{1,0:T(8,128)S(1)}, f32[512,32]{1,0:T(8,128)}, u32[]{:S(2)}) copy-start(f32[512,32]{1,0:T(8,128)} %get-tuple-element.12.raw_ref) | copy-start | bytes 196612
  6.5 8.5 %copy-start.3 = (f32[16]{0:T(128)S(1)}, f32[16]{0:T(128)}, u32[]{:S(2)}) copy-start(f32[16]{0:T(128)} %param.13) | copy-start | bytes 196
  6.5 8.5 %copy-start.4 = (f32[16]{0:T(128)S(1)}, f32[16]{0:T(128)}, u32[]{:S(2)}) copy-start(f32[16]{0:T(128)} %param.14) | copy-start | bytes 196

commit v6 on v5

--- a/solution.py
+++ b/solution.py
@@ -38,15 +38,17 @@
 
 
 def gather_kernel(n, tokens_ref, bc_ref, dt_ref, bias_ref, whole_ref, both_ref, raw_ref, *scratch):
-    columns, dt, send_bc, recv_bc, send_tok, recv_tok, here_sem = scratch
+    columns, dt, mine, came, send_bc, recv_bc, send_tok, recv_tok, here_sem, back_sem = scratch
     me = lax.axis_index("tp")
-    width = tokens_ref.shape[1]
+    length, width = tokens_ref.shape
+    bands = [pl.ds(r * (length // 2), length // 2) for r in range(2)]
 
     def features(owner):
         return pl.ds(pl.multiple_of(owner * width, width), width)
 
     own_bc = pltpu.make_async_copy(bc_ref, columns.at[me], here_sem.at[0])
-    own_tokens = pltpu.make_async_copy(tokens_ref, whole_ref.at[:, features(me)], here_sem.at[1])
+    own_tokens = pltpu.make_async_copy(tokens_ref, mine, here_sem.at[1])
+    own_part = pltpu.make_async_copy(tokens_ref, whole_ref.at[:, features(me)], here_sem.at[3])
     own_dt = pltpu.make_async_copy(dt_ref, dt, here_sem.at[2])
     barrier = pltpu.get_barrier_semaphore()
     for d in range(1, n):
@@ -70,35 +72,52 @@
                 device_id_type=pl.DeviceIdType.MESH,
             )
         )
-        parts.append(
-            pltpu.make_async_remote_copy(
-                src_ref=tokens_ref,
-                dst_ref=whole_ref.at[:, features(me)],
-                send_sem=send_tok.at[d - 1],
-                recv_sem=recv_tok.at[d - 1],
-                device_id=to,
-                device_id_type=pl.DeviceIdType.MESH,
+        for r, band in enumerate(bands):
+            parts.append(
+                pltpu.make_async_remote_copy(
+                    src_ref=tokens_ref.at[band, :],
+                    dst_ref=came.at[d - 1, band, :],
+                    send_sem=send_tok.at[2 * d - 2 + r],
+                    recv_sem=recv_tok.at[2 * d - 2 + r],
+                    device_id=to,
+                    device_id_type=pl.DeviceIdType.MESH,
+                )
             )
-        )
     for copy in weights + parts:
         copy.start()
+    own_part.start()
     own_bc.wait()
     own_tokens.wait()
     own_dt.wait()
     for copy in weights:
         copy.wait()
-    both = None
-    raw = jnp.concatenate([bias_ref[:1, :], bias_ref[1:, :]], axis=1)
-    for d in range(n):
-        if d:
-            parts[d - 1].wait()
-        here = features((me + n - d) % n)
-        part = whole_ref[:, here]
+
+    def products(part, owner):
+        here = features(owner)
         new = jnp.concatenate([dot(part, columns[s, here, :]) for s in range(n)], axis=1)
-        both = new if both is None else both + new
-        raw = raw + dot(part, dt[:, here], ((1,), (1,)))
-    both_ref[...] = both.astype(BF16)
-    raw_ref[...] = raw
+        return new, dot(part, dt[:, here], ((1,), (1,)))
+
+    own_both, own_raw = products(mine[...], me)
+    bias = jnp.concatenate([bias_ref[:1, :], bias_ref[1:, :]], axis=1)
+    backs = [own_part]
+    for r, band in enumerate(bands):
+        both = own_both[r * (length // 2) : (r + 1) * (length // 2), :]
+        raw = own_raw[r * (length // 2) : (r + 1) * (length // 2), :] + bias
+        for d in range(1, n):
+            owner = (me + n - d) % n
+            slot = 2 * d - 2 + r
+            parts[slot].wait()
+            source = came.at[d - 1, band, :]
+            target = whole_ref.at[band, features(owner)]
+            backs.append(pltpu.make_async_copy(source, target, back_sem.at[slot]))
+            backs[-1].start()
+            new_both, new_raw = products(came[d - 1, band, :], owner)
+            both = both + new_both
+            raw = raw + new_raw
+        both_ref[band, :] = both.astype(BF16)
+        raw_ref[band, :] = raw
+    for copy in backs:
+        copy.wait()
 
 
 def mixer_kernel(
@@ -442,13 +461,16 @@
             jax.ShapeDtypeStruct((length, 2 * heads), F32),
         ),
         in_specs=[pl.BlockSpec(memory_space=pltpu.HBM)] * 3 + [vmem],
-        out_specs=(vmem, vmem, vmem),
+        out_specs=(anywhere, vmem, vmem),
         scratch_shapes=[
             pltpu.VMEM((n,) + bc_weight.shape, BF16),
             pltpu.VMEM((2 * heads, features), BF16),
+            pltpu.VMEM(tokens.shape, BF16),
+            pltpu.VMEM((n - 1,) + tokens.shape, BF16),
         ]
-        + [dma((n - 1,))] * 4
-        + [dma((3,))],
+        + [dma((n - 1,))] * 2
+        + [dma((2 * (n - 1),))] * 2
+        + [dma((4,)), dma((2 * (n - 1),))],
         compiler_params=pltpu.CompilerParams(
             vmem_limit_bytes=GATHER_LIMIT, collective_id=0, has_side_effects=True
         ),

time: 46.5 us -> 75.2 us (1.62)
  Pallas kernels: 36.3 us -> 65 us
    pallas_call x1, Pallas kernels: 6.42 us -> 34.9 us  [shards(): pl.pallas_call(functools.partial(gather_kernel, n), out_shape=(jax.ShapeD...]
where the time goes in v6:
time: 75.2 us; the launch traced here: 75 us
  Pallas kernels  65 us (86%)
  matrix products  8.48 us (11%)
  other arithmetic  1.37 us (2%)
    pallas_call x1, Pallas kernels, shards(): pl.pallas_call(functools.partial(gather_kernel, n), out_shape=(jax.ShapeD...  34.9 us
    pallas_call x1, Pallas kernels, shards(): pl.pallas_call(functools.partial(mixer_kernel, outer, n), out_shape=(jax....  30.1 us
    dot_general x1, matrix products, shards(): jnp.einsum('td,dkf->ktf', whole, in_weight, preferred_element_type=F32)  8.48 us

profile of v6, /device:TPU:0, one launch (start us, length us, event | category | flops | bytes accessed | tf_op | source)
XLA Modules:
  0.0 75.0 jit_solution(15255228098967048810)
XLA Ops:
  0.0 34.9 %gather_features.1 = (bf16[512,2048]{1,0:T(8,128)(2,1)}, bf16[512,256]{1,0:T(8,128)(2,1)}, f32[512,32]{1,0:T(8,128)}) custom-call(bf16[512,1024]{1,0:T(8,128)(2,1)} %tokens_ref.1, bf16[2048,128]{1,0:T(8,128)(2,1)} %bc_ref.1, bf16[32,2048]{1,0:T(8,128)(2,1)} %bitcast.15, f32[2,16]{1,0:T(2,128)} %bias_ref.1), custom_call_target="tpu_custom_call" | custom-call | tf_op jit(solution)/shard_map/gather_features/pallas_call | solution.py:456
  34.9 0.0 copy-start
  34.9 0.0 copy-start.1
  34.9 0.0 copy-start.2
  34.9 0.0 copy-start.3
  35.0 0.0 copy-start.4
  35.0 8.5 %fusion.2.proj_ref = f32[2,512,1024]{2,1,0:T(8,128)S(1)} fusion(bf16[2048,2,1024]{2,1,0:T(2,128)(2,1)} %param.9, bf16[512,2048]{1,0:T(8,128)(2,1)} %get-tuple-element.10), kind=kOutput, calls=%fused_computation.2 | convolution fusion | flops 4294967296 | bytes 14680064 | tf_op jit(solution)/shard_map/td,dkf->ktf/dot_general | solution.py:484
  43.5 0.0 copy-done
  43.5 0.0 copy-done.1
  43.5 0.0 copy-done.2
  43.5 0.0 copy-done.3
  43.5 0.0 copy-done.4
  43.5 30.1 %mixer.1 = (bf16[512,1024]{1,0:T(8,128)(2,1)S(1)}, bf16[1,512,1024]{2,1,0:T(8,128)(2,1)S(1)}) custom-call(f32[2,512,1024]{2,1,0:T(8,128)S(1)} %fusion.2.proj_ref, bf16[512,256]{1,0:T(8,128)(2,1)S(1)} %copy-done.1, f32[512,32]{1,0:T(8,128)S(1)} %copy-done.2, f32[1,16]{1,0:T(1,128)S(1)} %bitcast.13, f32[1,16]{1,0:T(1,128)S(1)} %bitcast.14, ...), custom_call_target="tpu_custom_call" | custom-call | tf_op jit(solution)/shard_map/mixer/pallas_call | solution.py:485
  73.6 1.4 %fusion.5 = bf16[512,1024]{1,0:T(8,128)(2,1)} fusion(bf16[512,1024]{1,0:T(8,128)(2,1)S(1)} %get-tuple-element.13, bf16[1,512,1024]{2,1,0:T(8,128)(2,1)S(1)} %get-tuple-element.14), kind=kLoop, calls=%fused_computation.4 | loop fusion | flops 2097152 | bytes 3145728 | tf_op jit(solution)/shard_map/convert_element_type | solution.py:529
Async XLA Ops:
  34.9 8.5 %copy-start = (bf16[1024,2048]{1,0:T(8,128)(2,1)S(1)}, bf16[1024,2048]{1,0:T(8,128)(2,1)}, u32[]{:S(2)}) copy-start(bf16[1024,2048]{1,0:T(8,128)(2,1)} %weight_hbm.1) | copy-start | bytes 12582916
  34.9 8.5 %copy-start.1 = (bf16[512,256]{1,0:T(8,128)(2,1)S(1)}, bf16[512,256]{1,0:T(8,128)(2,1)}, u32[]{:S(2)}) copy-start(bf16[512,256]{1,0:T(8,128)(2,1)} %get-tuple-element.11.both_ref) | copy-start | bytes 786436
  34.9 8.5 %copy-start.2 = (f32[512,32]{1,0:T(8,128)S(1)}, f32[512,32]{1,0:T(8,128)}, u32[]{:S(2)}) copy-start(f32[512,32]{1,0:T(8,128)} %get-tuple-element.12.raw_ref) | copy-start | bytes 196612
  34.9 8.5 %copy-start.3 = (f32[16]{0:T(128)S(1)}, f32[16]{0:T(128)}, u32[]{:S(2)}) copy-start(f32[16]{0:T(128)} %param.13) | copy-start | bytes 196
  35.0 8.5 %copy-start.4 = (f32[16]{0:T(128)S(1)}, f32[16]{0:T(128)}, u32[]{:S(2)}) copy-start(f32[16]{0:T(128)} %param.14) | copy-start | bytes 196

commit v7 on v6

--- a/solution.py
+++ b/solution.py
@@ -48,7 +48,7 @@
 
     own_bc = pltpu.make_async_copy(bc_ref, columns.at[me], here_sem.at[0])
     own_tokens = pltpu.make_async_copy(tokens_ref, mine, here_sem.at[1])
-    own_part = pltpu.make_async_copy(tokens_ref, whole_ref.at[:, features(me)], here_sem.at[3])
+    own_part = pltpu.make_async_copy(mine, whole_ref.at[:, features(me)], here_sem.at[3])
     own_dt = pltpu.make_async_copy(dt_ref, dt, here_sem.at[2])
     barrier = pltpu.get_barrier_semaphore()
     for d in range(1, n):
@@ -85,9 +85,9 @@
             )
     for copy in weights + parts:
         copy.start()
+    own_tokens.wait()
     own_part.start()
     own_bc.wait()
-    own_tokens.wait()
     own_dt.wait()
     for copy in weights:
         copy.wait()

time: 75.2 us -> 46.4 us (0.62)
  Pallas kernels: 65 us -> 36.2 us
    pallas_call x1, Pallas kernels: 34.9 us -> 6.33 us  [shards(): pl.pallas_call(functools.partial(gather_kernel, n), out_shape=(jax.ShapeD...]
where the time goes in v7:
time: 46.4 us; the launch traced here: 46.2 us
  Pallas kernels  36.2 us (78%)
  matrix products  8.48 us (18%)
  other arithmetic  1.37 us (3%)
    pallas_call x1, Pallas kernels, shards(): pl.pallas_call(functools.partial(mixer_kernel, outer, n), out_shape=(jax....  29.9 us
    dot_general x1, matrix products, shards(): jnp.einsum('td,dkf->ktf', whole, in_weight, preferred_element_type=F32)  8.48 us
    pallas_call x1, Pallas kernels, shards(): pl.pallas_call(functools.partial(gather_kernel, n), out_shape=(jax.ShapeD...  6.33 us
    convert_element_type x1, other arithmetic, shards(): return total.astype(BF16)  1.37 us

profile of v7, /device:TPU:0, one launch (start us, length us, event | category | flops | bytes accessed | tf_op | source)
XLA Modules:
  0.0 46.2 jit_solution(11464273186059156030)
XLA Ops:
  0.0 6.3 %gather_features.1 = (bf16[512,2048]{1,0:T(8,128)(2,1)}, bf16[512,256]{1,0:T(8,128)(2,1)}, f32[512,32]{1,0:T(8,128)}) custom-call(bf16[512,1024]{1,0:T(8,128)(2,1)} %tokens_ref.1, bf16[2048,128]{1,0:T(8,128)(2,1)} %bc_ref.1, bf16[32,2048]{1,0:T(8,128)(2,1)} %bitcast.15, f32[2,16]{1,0:T(2,128)} %bias_ref.1), custom_call_target="tpu_custom_call" | custom-call | tf_op jit(solution)/shard_map/gather_features/pallas_call | solution.py:456
  6.3 0.0 copy-start
  6.4 0.0 copy-start.1
  6.4 0.0 copy-start.2
  6.4 0.0 copy-start.3
  6.4 0.0 copy-start.4
  6.4 8.5 %fusion.2.proj_ref = f32[2,512,1024]{2,1,0:T(8,128)S(1)} fusion(bf16[2048,2,1024]{2,1,0:T(2,128)(2,1)} %param.9, bf16[512,2048]{1,0:T(8,128)(2,1)} %get-tuple-element.10), kind=kOutput, calls=%fused_computation.2 | convolution fusion | flops 4294967296 | bytes 14680064 | tf_op jit(solution)/shard_map/td,dkf->ktf/dot_general | solution.py:484
  14.9 0.0 copy-done
  14.9 0.0 copy-done.1
  14.9 0.0 copy-done.2
  14.9 0.0 copy-done.3
  14.9 0.0 copy-done.4
  14.9 29.9 %mixer.1 = (bf16[512,1024]{1,0:T(8,128)(2,1)S(1)}, bf16[1,512,1024]{2,1,0:T(8,128)(2,1)S(1)}) custom-call(f32[2,512,1024]{2,1,0:T(8,128)S(1)} %fusion.2.proj_ref, bf16[512,256]{1,0:T(8,128)(2,1)S(1)} %copy-done.1, f32[512,32]{1,0:T(8,128)S(1)} %copy-done.2, f32[1,16]{1,0:T(1,128)S(1)} %bitcast.13, f32[1,16]{1,0:T(1,128)S(1)} %bitcast.14, ...), custom_call_target="tpu_custom_call" | custom-call | tf_op jit(solution)/shard_map/mixer/pallas_call | solution.py:485
  44.8 1.4 %fusion.5 = bf16[512,1024]{1,0:T(8,128)(2,1)} fusion(bf16[512,1024]{1,0:T(8,128)(2,1)S(1)} %get-tuple-element.13, bf16[1,512,1024]{2,1,0:T(8,128)(2,1)S(1)} %get-tuple-element.14), kind=kLoop, calls=%fused_computation.4 | loop fusion | flops 2097152 | bytes 3145728 | tf_op jit(solution)/shard_map/convert_element_type | solution.py:529
Async XLA Ops:
  6.3 8.5 %copy-start = (bf16[1024,2048]{1,0:T(8,128)(2,1)S(1)}, bf16[1024,2048]{1,0:T(8,128)(2,1)}, u32[]{:S(2)}) copy-start(bf16[1024,2048]{1,0:T(8,128)(2,1)} %weight_hbm.1) | copy-start | bytes 12582916
  6.4 8.5 %copy-start.1 = (bf16[512,256]{1,0:T(8,128)(2,1)S(1)}, bf16[512,256]{1,0:T(8,128)(2,1)}, u32[]{:S(2)}) copy-start(bf16[512,256]{1,0:T(8,128)(2,1)} %get-tuple-element.11.both_ref) | copy-start | bytes 786436
  6.4 8.5 %copy-start.2 = (f32[512,32]{1,0:T(8,128)S(1)}, f32[512,32]{1,0:T(8,128)}, u32[]{:S(2)}) copy-start(f32[512,32]{1,0:T(8,128)} %get-tuple-element.12.raw_ref) | copy-start | bytes 196612
  6.4 8.5 %copy-start.3 = (f32[16]{0:T(128)S(1)}, f32[16]{0:T(128)}, u32[]{:S(2)}) copy-start(f32[16]{0:T(128)} %param.13) | copy-start | bytes 196
  6.4 8.5 %copy-start.4 = (f32[16]{0:T(128)S(1)}, f32[16]{0:T(128)}, u32[]{:S(2)}) copy-start(f32[16]{0:T(128)} %param.14) | copy-start | bytes 196
